TPU v7x, 128 devices: a whole 4x4x4 slice. The times are simulated.
128 devices in a mesh: gx: 16 (over y_lo, z, core), gy: 8 (over y_hi, x).
Axes of the slice: x: 4, y: 4 (y_hi: 2, y_lo: 2; y = y_hi * 2 + y_lo), z: 4, core: 2. Of those that a mesh axis runs over, the one named last changes fastest.
Arguments:
- populations: float32 [19, 256, 128, 512], P(None, 'gx', 'gy'), may hold values from 0.001 to 1.3
- solid: int32 [256, 128, 512], P('gx', 'gy'), may hold values from 0 to 1
- counts: float32 [64, 32, 16, 64], P(None, 'gx', None, 'gy'), may hold values from 0.02 to 45
- breakage: float32 [64, 64], replicated, may hold values from 0 to 4, as said below
- selection: float32 [64], replicated, may hold values from 0.05 to 1
Outputs:
- read: float32 [19, 256, 128, 512], P(None, 'gx', 'gy')
- counts_next: float32 [64, 32, 16, 64], P(None, 'gx', None, 'gy')
Inputs may be any that keep to these rules, and one draw needn't show every extreme that they name: breakage is zero on and below the diagonal.
All inputs are finite; a program needn't handle non-finite values.
Results may differ from a plain program's by a relative error of at most 0.0001.
Values sent between devices are 32-bit elements; how exact they have to be, the bound alone decides.
A program may use at most 192 MiB of HBM per device.

v0:
```python
import jax
import jax.numpy as jnp
from jax import lax
from jax.sharding import PartitionSpec as P

SUB = 4


velocities = (
    (0, 0, 0),
    (1, 0, 0),
    (-1, 0, 0),
    (0, 1, 0),
    (0, -1, 0),
    (0, 0, 1),
    (0, 0, -1),
    (1, 1, 0),
    (-1, -1, 0),
    (1, -1, 0),
    (-1, 1, 0),
    (1, 0, 1),
    (-1, 0, -1),
    (1, 0, -1),
    (-1, 0, 1),
    (0, 1, 1),
    (0, -1, -1),
    (0, 1, -1),
    (0, -1, 1),
)
lattice_weights = (1.0 / 3.0,) + (1.0 / 18.0,) * 6 + (1.0 / 36.0,) * 12
opposite = (0, 2, 1, 4, 3, 6, 5, 8, 7, 10, 9, 12, 11, 14, 13, 16, 15, 18, 17)


def with_halo(cells, sides, width):
    for axis, dim in sides:
        count = lax.axis_size(axis)
        head = lax.slice_in_dim(cells, 0, width, axis=dim)
        tail = lax.slice_in_dim(cells, cells.shape[dim] - width, cells.shape[dim], axis=dim)
        cells = jnp.concatenate(
            [
                lax.ppermute(tail, axis, [(i, (i + 1) % count) for i in range(count)]),
                cells,
                lax.ppermute(head, axis, [((i + 1) % count, i) for i in range(count)]),
            ],
            axis=dim,
        )
    return cells


def expand(coarse):
    a, b, c = coarse.shape
    return jnp.broadcast_to(coarse[:, None, :, None, :, None], (a, 8, b, 8, c, 8)).reshape(
        a * 8, b * 8, c * 8
    )


def block_mean(field):
    a, b, c = field.shape
    return field.reshape(a // 8, 8, b // 8, 8, c // 8, 8).sum(axis=(1, 3, 5)) / 512.0


def relax_time(counts):
    classes = counts.shape[0]
    volume = (jnp.arange(classes).astype(jnp.float32) + 1.0) / classes
    load = jnp.sum(volume[:, None, None, None] * counts, axis=0)
    packed = 0.5 * load / (1.0 + load)
    thinned = 1.0 - packed / 0.64
    return 0.5 + 3.0 * (0.04 / (thinned * thinned))


def heat_factor(tau):
    return (tau - 0.5) / (3.0 * tau * tau)


def collide(populations, tau_fine, fluid):
    rho = populations[0]
    for index in range(1, 19):
        rho = rho + populations[index]
    moments = [jnp.zeros_like(rho), jnp.zeros_like(rho), jnp.zeros_like(rho)]
    for index, vector in enumerate(velocities):
        for axis_num in range(3):
            if vector[axis_num] != 0:
                moments[axis_num] = moments[axis_num] + vector[axis_num] * populations[index]
    vel_x = moments[0] / rho
    vel_y = moments[1] / rho
    vel_z = moments[2] / rho
    speed_sq = vel_x * vel_x + vel_y * vel_y + vel_z * vel_z
    stress = [jnp.zeros_like(rho) for slot in range(6)]
    pairs = ((0, 0), (1, 1), (2, 2), (0, 1), (0, 2), (1, 2))
    posted = []
    for index, vector in enumerate(velocities):
        along = vector[0] * vel_x + vector[1] * vel_y + vector[2] * vel_z
        equil = (
            lattice_weights[index]
            * rho
            * (1.0 + 3.0 * along + 4.5 * along * along - 1.5 * speed_sq)
        )
        noneq = populations[index] - equil
        for slot, pair in enumerate(pairs):
            factor = vector[pair[0]] * vector[pair[1]]
            if factor != 0:
                stress[slot] = stress[slot] + factor * noneq
        posted.append(populations[index] - noneq / tau_fine)
    post = jnp.stack(
        [jnp.where(fluid, posted[index], populations[opposite[index]]) for index in range(19)]
    )
    square = stress[0] * stress[0] + stress[1] * stress[1] + stress[2] * stress[2]
    square = square + 2.0 * (stress[3] * stress[3] + stress[4] * stress[4] + stress[5] * stress[5])
    heat = jnp.where(fluid, 4.5 * square / (rho * rho), 0.0)
    return (post, heat)


def per_device(populations, solid, counts, breakage, selection):
    tau_owner = relax_time(counts)
    tau_tile = lax.all_to_all(tau_owner, "gy", split_axis=1, concat_axis=2, tiled=True)
    tau_fine = expand(tau_tile)
    post, heat = collide(populations, tau_fine, solid == 0)
    eps = lax.all_to_all(
        block_mean(heat * heat_factor(tau_fine)), "gy", split_axis=2, concat_axis=1, tiled=True
    )
    width_x = post.shape[1]
    width_y = post.shape[2]
    padded = with_halo(post, (("gx", 1), ("gy", 2)), 1)
    moved = []
    for index, vector in enumerate(velocities):
        start_x = 1 - vector[0]
        start_y = 1 - vector[1]
        window = padded[index, start_x : start_x + width_x, start_y : start_y + width_y]
        moved.append(jnp.roll(window, vector[2], axis=2))
    read = jnp.stack(moved)
    strength = jnp.sqrt(50.0 * eps + 1e-06)
    gain_flat = (strength / (1.0 + strength)).reshape(1, -1)
    rate = selection[:, None] * gain_flat
    classes = counts.shape[0]
    current = counts.reshape(classes, -1)
    for step in range(SUB):
        lost = rate * current
        born = jnp.dot(
            breakage, lost, precision=lax.Precision.HIGHEST, preferred_element_type=jnp.float32
        )
        current = current + 0.25 * (born - lost)
    return (read, current.reshape(counts.shape))


def solution(mesh):
    in_specs = (P(None, "gx", "gy", None), P("gx", "gy", None), P(None, "gx", None, "gy"), P(), P())
    out_specs = (P(None, "gx", "gy", None), P(None, "gx", None, "gy"))
    return jax.shard_map(
        per_device, mesh=mesh, in_specs=in_specs, out_specs=out_specs, check_vma=False
    )
```

profile of v0, /device:TPU:0, one launch (start us, length us, event | category | flops | bytes accessed | tf_op | source)
XLA Modules:
  0.0 143.4 jit_solution(3811326352655777197)
XLA Ops:
  0.7 1.0 multiply_reduce_fusion
  2.5 7.0 %all-to-all-start = ((f32[2,16,8]{2,0,1:T(2,128)}), f32[2,16,8]{2,0,1:T(2,128)S(1)}, u32[]{:S(2)}, u32[]{:S(2)}) async-start(f32[2,16,8]{2,0,1:T(2,128)} %copy.35), calls=%async_computation | async-start | bytes 32768 | tf_op jit(solution)/shard_map/all_to_all | solution.py:115
  10.5 6.7 %all-to-all-done = f32[2,16,8]{2,0,1:T(2,128)S(1)} async-done(((f32[2,16,8]{2,0,1:T(2,128)}), f32[2,16,8]{2,0,1:T(2,128)S(1)}, u32[]{:S(2)}, u32[]{:S(2)}) %all-to-all-start) | async-done | bytes 1056 | tf_op jit(solution)/shard_map/all_to_all | solution.py:115
  17.3 4.5 %broadcast_in_dim.7 = f32[2,8,2,8,64,8]{5,4,3,2,1,0:T(8,128)} broadcast(f32[2,2,64]{2,1,0:T(2,128)S(1)} %broadcast_in_dim.5), dimensions={0,2,4} | broadcast | bytes 525312 | tf_op jit(solution)/shard_map/broadcast_in_dim | solution.py:52
  21.8 6.9 %reshape.44 = f32[16,16,512]{2,1,0:T(8,128)S(1)} reshape(f32[2,8,2,8,64,8]{5,4,3,2,1,0:T(8,128)} %broadcast_in_dim.7) | data formatting | bytes 1048576 | tf_op jit(solution)/shard_map/reshape | solution.py:52
  28.7 13.1 %fusion.90 = (f32[16,16,512]{2,1,0:T(8,128)}, f32[16,16,512]{2,1,0:T(8,128)}, f32[16,16,512]{2,1,0:T(8,128)}, f32[16,16,512]{2,1,0:T(8,128)}, f32[16,16,512]{2,1...) fusion(f32[16,16,512]{2,1,0:T(8,128)S(1)} %reshape.44, ...), kind=kLoop, calls=%fused_computation.118 | loop fusion | flops 40501248 | bytes 23724032 | tf_op jit(solution)/shard_map/mul | solution.py:119
  41.8 7.0 %reshape.46 = f32[2,8,2,8,64,8]{5,4,3,2,1,0:T(8,128)} reshape(f32[16,16,512]{2,1,0:T(8,128)} %get-tuple-element.4) | data formatting | bytes 1048576 | tf_op jit(solution)/shard_map/reshape | solution.py:59
  48.8 4.2 %reduce_sum.19 = f32[2,2,64]{2,1,0:T(2,128)S(1)} reduce(f32[2,8,2,8,64,8]{5,4,3,2,1,0:T(8,128)} %reshape.46, f32[]{:T(128)} %constant.23.clone.1), dimensions={1,3,5}, to_apply=%region_1.2 | reduce | flops 130816 | bytes 525316 | tf_op jit(solution)/shard_map/reduce_sum | solution.py:59
  53.7 4.2 %all-to-all-start.1 = ((f32[2,2,64]{1,0,2:T(2,128)}), f32[2,2,64]{1,0,2:T(2,128)}, u32[]{:S(2)}, u32[]{:S(2)}) async-start(f32[2,2,64]{1,0,2:T(2,128)} %copy.38), calls=%async_computation.1 | async-start | bytes 131072 | tf_op jit(solution)/shard_map/all_to_all | solution.py:118
  57.9 1.8 %bitcast_dynamic-update-slice_fusion.18 = f32[19,16,16,512]{3,2,1,0:T(8,128)S(1)} fusion(pred[16,16,512]{2,1,0:T(8,128)(4,1)S(1)} %get-tuple-element.28, f32[16,16,512]{2,1,0:T(8,128)S(1)} %reshape.44, f32[16,16,512]{2,1,0:T(8,128)S(1)} %get-tuple-element.23, f32[16,16,512]{2,1,0:T(8,128)} %get-tuple-element.26, f32[16,16,512]{2,1,0:T(8,128)S(1)} %get-tuple-element.25, ...), kind=kLoop, calls=%fused_computation.181 | loop fusion | flops 2228223 | bytes 4325376
  59.8 4.0 %copy.62 = f32[19,16,16,512]{3,2,1,0:T(8,128)} copy(f32[19,16,16,512]{3,2,1,0:T(8,128)S(1)} %bitcast_dynamic-update-slice_fusion.18) | data formatting | bytes 19922944
  63.8 1.6 %bitcast_dynamic-update-slice_fusion.17 = f32[19,16,16,512]{3,2,1,0:T(8,128)S(1)} fusion(f32[19,16,16,512]{3,2,1,0:T(8,128)S(1)} %bitcast_dynamic-update-slice_fusion.18, pred[16,16,512]{2,1,0:T(8,128)(4,1)S(1)} %get-tuple-element.28, f32[16,16,512]{2,1,0:T(8,128)S(1)} %copy-done.18, f32[16,16,512]{2,1,0:T(8,128)S(1)} %reshape.44, f32[19,16,16,512]{3,2,1,0:T(8,128)} %param.5), kind=kLoop, calls=%fused_computation.180 | loop fusion | flops 393216 | bytes 2752512
  65.4 1.7 %bitcast_dynamic-update-slice_fusion.16 = f32[19,16,16,512]{3,2,1,0:T(8,128)S(1)} fusion(f32[19,16,16,512]{3,2,1,0:T(8,128)S(1)} %bitcast_dynamic-update-slice_fusion.17, pred[16,16,512]{2,1,0:T(8,128)(4,1)S(1)} %get-tuple-element.28, f32[16,16,512]{2,1,0:T(8,128)S(1)} %copy-done.17, f32[16,16,512]{2,1,0:T(8,128)S(1)} %reshape.44, f32[19,16,16,512]{3,2,1,0:T(8,128)} %param.5), kind=kLoop, calls=%fused_computation.179 | loop fusion | flops 393216 | bytes 2752512
  67.2 1.6 %bitcast_dynamic-update-slice_fusion.15 = f32[19,16,16,512]{3,2,1,0:T(8,128)S(1)} fusion(f32[19,16,16,512]{3,2,1,0:T(8,128)S(1)} %bitcast_dynamic-update-slice_fusion.16, pred[16,16,512]{2,1,0:T(8,128)(4,1)S(1)} %get-tuple-element.28, f32[16,16,512]{2,1,0:T(8,128)S(1)} %copy-done.16, f32[16,16,512]{2,1,0:T(8,128)S(1)} %reshape.44, f32[19,16,16,512]{3,2,1,0:T(8,128)} %param.5), kind=kLoop, calls=%fused_computation.178 | loop fusion | flops 393216 | bytes 2752512
  68.8 1.6 %bitcast_dynamic-update-slice_fusion.14 = f32[19,16,16,512]{3,2,1,0:T(8,128)S(1)} fusion(f32[19,16,16,512]{3,2,1,0:T(8,128)S(1)} %bitcast_dynamic-update-slice_fusion.15, pred[16,16,512]{2,1,0:T(8,128)(4,1)S(1)} %get-tuple-element.28, f32[16,16,512]{2,1,0:T(8,128)S(1)} %copy-done.15, f32[16,16,512]{2,1,0:T(8,128)S(1)} %reshape.44, f32[19,16,16,512]{3,2,1,0:T(8,128)} %param.5), kind=kLoop, calls=%fused_computation.177 | loop fusion | flops 393216 | bytes 2752512
  70.4 1.5 %bitcast_dynamic-update-slice_fusion.13 = (f32[19,16,16,512]{3,2,1,0:T(8,128)S(1)}, f32[16,16,512]{2,1,0:T(8,128)S(1)}) fusion(f32[19,16,16,512]{3,2,1,0:T(8,128)S(1)} %bitcast_dynamic-update-slice_fusion.14, pred[16,16,512]{2,1,0:T(8,128)(4,1)S(1)} %get-tuple-element.28, f32[19,16,16,512]{3,2,1,0:T(8,128)} %param.5, ...), kind=kLoop, calls=%fused_computation.176 | loop fusion | flops 393216 | bytes 3276800
  71.9 1.6 %bitcast_dynamic-update-slice_fusion.12 = (f32[19,16,16,512]{3,2,1,0:T(8,128)S(1)}, f32[16,16,512]{2,1,0:T(8,128)S(1)}) fusion(f32[19,16,16,512]{3,2,1,0:T(8,128)S(1)} %get-tuple-element.31, pred[16,16,512]{2,1,0:T(8,128)(4,1)S(1)} %get-tuple-element.28, f32[19,16,16,512]{3,2,1,0:T(8,128)} %param.5, f32[16,16,512]{2,1,0:T(8,128)S(1)} %get-tuple-element.17, ...), kind=kLoop, calls=%fused_computation.175 | loop fusion | flops 393216 | bytes 3276800
  73.5 1.5 %bitcast_dynamic-update-slice_fusion.11 = f32[19,16,16,512]{3,2,1,0:T(8,128)S(1)} fusion(f32[19,16,16,512]{3,2,1,0:T(8,128)S(1)} %get-tuple-element.29, pred[16,16,512]{2,1,0:T(8,128)(4,1)S(1)} %get-tuple-element.28, f32[16,16,512]{2,1,0:T(8,128)S(1)} %copy-done.14, f32[16,16,512]{2,1,0:T(8,128)S(1)} %reshape.44, f32[19,16,16,512]{3,2,1,0:T(8,128)} %param.5), kind=kLoop, calls=%fused_computation.174 | loop fusion | flops 393216 | bytes 2752512
  75.0 1.5 %bitcast_dynamic-update-slice_fusion.10 = f32[19,16,16,512]{3,2,1,0:T(8,128)S(1)} fusion(f32[19,16,16,512]{3,2,1,0:T(8,128)S(1)} %bitcast_dynamic-update-slice_fusion.11, pred[16,16,512]{2,1,0:T(8,128)(4,1)S(1)} %get-tuple-element.28, f32[16,16,512]{2,1,0:T(8,128)S(1)} %copy-done.13, f32[16,16,512]{2,1,0:T(8,128)S(1)} %reshape.44, f32[19,16,16,512]{3,2,1,0:T(8,128)} %param.5), kind=kLoop, calls=%fused_computation.173 | loop fusion | flops 393216 | bytes 2752512
  79.3 3.8 %copy-done.1 = f32[19,16,16,512]{3,2,1,0:T(8,128)} copy-done((f32[19,16,16,512]{3,2,1,0:T(8,128)}, f32[19,16,16,512]{3,2,1,0:T(8,128)S(1)}, u32[]{:S(2)}) %copy-start.1) | copy-done | bytes 9961496
  83.3 1.0 slice.347
  84.4 2.2 %collective-permute-start.1 = (f32[19,1,16,512]{3,2,1,0:T(8,128)S(1)}, f32[19,1,16,512]{3,2,1,0:T(8,128)S(1)}, u32[]{:S(2)}, u32[]{:S(2)}) collective-permute-start(f32[19,1,16,512]{3,2,1,0:T(8,128)S(1)} %get-tuple-element.45), channel_id=1, source_target_pairs={{8,0},{16,8},{24,16},{32,24},{40,32},{48,40},{56,48},{64,56},{72,6... | collective-permute-start | bytes 1867784 | tf_op jit(solution)/shard_map/ppermute | solution.py:43
  88.3 6.0 %collective-permute-done.1 = f32[19,1,16,512]{3,2,1,0:T(8,128)S(1)} collective-permute-done((f32[19,1,16,512]{3,2,1,0:T(8,128)S(1)}, f32[19,1,16,512]{3,2,1,0:T(8,128)S(1)}, u32[]{:S(2)}, u32[]{:S(2)}) %collective-permute-start.1) | collective-permute-done | bytes 622624 | tf_op jit(solution)/shard_map/ppermute | solution.py:43
  94.4 4.0 %collective-permute-done = f32[19,1,16,512]{3,2,1,0:T(8,128)S(1)} collective-permute-done((f32[19,1,16,512]{3,2,1,0:T(8,128)S(1)}, f32[19,1,16,512]{3,2,1,0:T(8,128)S(1)}, u32[]{:S(2)}, u32[]{:S(2)}) %collective-permute-start) | collective-permute-done | bytes 622624 | tf_op jit(solution)/shard_map/ppermute | solution.py:41
  98.4 5.4 %pad_maximum_fusion = (f32[19,18,1,512]{3,2,1,0:T(1,128)}, f32[19,18,1,512]{3,2,1,0:T(1,128)}) fusion(f32[19,1,16,512]{3,2,1,0:T(8,128)S(1)} %collective-permute-done.1, f32[19,16,16,512]{3,2,1,0:T(8,128)} %copy-done.1, f32[19,1,16,512]{3,2,1,0:T(8,128)S(1)} %collective-permute-done), kind=kLoop, calls=%fused_computation.37 | loop fusion | flops 700416 | bytes 12607488 | tf_op jit(solution)/shard_map/concatenate | solution.py:39
  103.7 5.7 %collective-permute-start.3 = (f32[19,18,1,512]{3,2,1,0:T(1,128)}, f32[19,18,1,512]{3,2,1,0:T(1,128)S(1)}, u32[]{:S(2)}, u32[]{:S(2)}) collective-permute-start(f32[19,18,1,512]{3,2,1,0:T(1,128)} %get-tuple-element.39), channel_id=1, source_target_pairs={{1,0},{2,1},{3,2},{4,3},{5,4},{6,5},{7,6},{0,7},{9,8},{10,9},{11,1... | collective-permute-start | bytes 2101256 | tf_op jit(solution)/shard_map/ppermute | solution.py:43
  110.7 2.0 %maximum_dynamic-update-slice_fusion.7 = f32[19,16,16,512]{3,2,1,0:T(8,128)} fusion(f32[19,16,16,512]{3,2,1,0:T(8,128)} %copy.62, f32[19,16,16,512]{3,2,1,0:T(8,128)} %copy-done.1, f32[19,1,16,512]{3,2,1,0:T(8,128)S(1)} %collective-permute-done), kind=kLoop, calls=%fused_computation.142 | loop fusion | flops 131072 | bytes 11108352
  112.8 2.6 %maximum_dynamic-update-slice_fusion.6 = f32[19,16,16,512]{3,2,1,0:T(8,128)} fusion(f32[19,16,16,512]{3,2,1,0:T(8,128)} %maximum_dynamic-update-slice_fusion.7, f32[19,1,16,512]{3,2,1,0:T(8,128)S(1)} %collective-permute-done.1, f32[19,16,16,512]{3,2,1,0:T(8,128)} %copy-done.1), kind=kLoop, calls=%fused_computation.141 | loop fusion | flops 131072 | bytes 11108352
  115.4 11.2 %collective-permute-done.2 = f32[19,18,1,512]{3,2,1,0:T(1,128)S(1)} collective-permute-done((f32[19,18,1,512]{3,2,1,0:T(1,128)}, f32[19,18,1,512]{3,2,1,0:T(1,128)S(1)}, u32[]{:S(2)}, u32[]{:S(2)}) %collective-permute-start.2) | collective-permute-done | bytes 700448 | tf_op jit(solution)/shard_map/ppermute | solution.py:41
  132.0 1.4 fusion.91
  133.4 1.1 fusion.92
  135.8 1.0 fusion.97
  (116 shorter events, 21.7 us)
Async XLA Ops:
  0.6 87.1 %copy-start = (f32[64,64]{1,0:T(8,128)S(1)}, f32[64,64]{1,0:T(8,128)}, u32[]{:S(2)}) copy-start(f32[64,64]{1,0:T(8,128)} %param.8) | copy-start | bytes 49156
  2.5 14.7 %all-to-all-start = ((f32[2,16,8]{2,0,1:T(2,128)}), f32[2,16,8]{2,0,1:T(2,128)S(1)}, u32[]{:S(2)}, u32[]{:S(2)}) async-start(f32[2,16,8]{2,0,1:T(2,128)} %copy.35), calls=%async_computation | async-start | bytes 32768 | tf_op jit(solution)/shard_map/all_to_all | solution.py:115
  53.7 32.9 %all-to-all-start.1 = ((f32[2,2,64]{1,0,2:T(2,128)}), f32[2,2,64]{1,0,2:T(2,128)}, u32[]{:S(2)}, u32[]{:S(2)}) async-start(f32[2,2,64]{1,0,2:T(2,128)} %copy.38), calls=%async_computation.1 | async-start | bytes 131072 | tf_op jit(solution)/shard_map/all_to_all | solution.py:118
  59.7 4.0 %copy-start.18 = (f32[16,16,512]{2,1,0:T(8,128)S(1)}, f32[16,16,512]{2,1,0:T(8,128)}, u32[]{:S(2)}) copy-start(f32[16,16,512]{2,1,0:T(8,128)} %get-tuple-element.22) | copy-start | bytes 1572868
  59.7 5.6 %copy-start.17 = (f32[16,16,512]{2,1,0:T(8,128)S(1)}, f32[16,16,512]{2,1,0:T(8,128)}, u32[]{:S(2)}) copy-start(f32[16,16,512]{2,1,0:T(8,128)} %get-tuple-element.21) | copy-start | bytes 1572868
  59.8 7.4 %copy-start.16 = (f32[16,16,512]{2,1,0:T(8,128)S(1)}, f32[16,16,512]{2,1,0:T(8,128)}, u32[]{:S(2)}) copy-start(f32[16,16,512]{2,1,0:T(8,128)} %get-tuple-element.20) | copy-start | bytes 1572868
  59.8 9.0 %copy-start.15 = (f32[16,16,512]{2,1,0:T(8,128)S(1)}, f32[16,16,512]{2,1,0:T(8,128)}, u32[]{:S(2)}) copy-start(f32[16,16,512]{2,1,0:T(8,128)} %get-tuple-element.19) | copy-start | bytes 1572868
  63.8 9.7 %copy-start.14 = (f32[16,16,512]{2,1,0:T(8,128)S(1)}, f32[16,16,512]{2,1,0:T(8,128)}, u32[]{:S(2)}) copy-start(f32[16,16,512]{2,1,0:T(8,128)} %get-tuple-element.16) | copy-start | bytes 1572868
  63.8 11.3 %copy-start.13 = (f32[16,16,512]{2,1,0:T(8,128)S(1)}, f32[16,16,512]{2,1,0:T(8,128)}, u32[]{:S(2)}) copy-start(f32[16,16,512]{2,1,0:T(8,128)} %get-tuple-element.15) | copy-start | bytes 1572868
  63.8 12.8 %slice-start.3 = ((s8[9961472]{0:T(1024)(128)(4,1)}), s8[4194304]{0:T(1024)(128)(4,1)S(1)}, s32[]{:S(2)}) async-start(s8[9961472]{0:T(1024)(128)(4,1)} %bitcast.525), calls=%async_computation.5 | async-start | bytes 8388608
  65.4 11.2 %copy-start.12 = (f32[16,16,512]{2,1,0:T(8,128)S(1)}, f32[16,16,512]{2,1,0:T(8,128)}, u32[]{:S(2)}) copy-start(f32[16,16,512]{2,1,0:T(8,128)} %get-tuple-element.14) | copy-start | bytes 1572868
  67.1 9.4 %slice-start.4 = ((s8[9961472]{0:T(1024)(128)(4,1)}), s8[4194304]{0:T(1024)(128)(4,1)S(1)}, s32[]{:S(2)}) async-start(s8[9961472]{0:T(1024)(128)(4,1)} %bitcast.525), calls=%async_computation.6 | async-start | bytes 8388608
  67.2 9.7 %copy-start.11 = (f32[16,16,512]{2,1,0:T(8,128)S(1)}, f32[16,16,512]{2,1,0:T(8,128)}, u32[]{:S(2)}) copy-start(f32[16,16,512]{2,1,0:T(8,128)} %get-tuple-element.13) | copy-start | bytes 1572868
  68.8 8.3 %copy-start.10 = (f32[16,16,512]{2,1,0:T(8,128)S(1)}, f32[16,16,512]{2,1,0:T(8,128)}, u32[]{:S(2)}) copy-start(f32[16,16,512]{2,1,0:T(8,128)} %get-tuple-element.12) | copy-start | bytes 1572868
  70.4 7.0 %copy-start.9 = (f32[16,16,512]{2,1,0:T(8,128)S(1)}, f32[16,16,512]{2,1,0:T(8,128)}, u32[]{:S(2)}) copy-start(f32[16,16,512]{2,1,0:T(8,128)} %get-tuple-element.11) | copy-start | bytes 1572868
  71.9 5.8 %copy-start.8 = (f32[16,16,512]{2,1,0:T(8,128)S(1)}, f32[16,16,512]{2,1,0:T(8,128)}, u32[]{:S(2)}) copy-start(f32[16,16,512]{2,1,0:T(8,128)} %get-tuple-element.10) | copy-start | bytes 1572868
  71.9 4.7 %slice-start.5 = ((s8[9961472]{0:T(1024)(128)(4,1)}), s8[1572864]{0:T(1024)(128)(4,1)S(1)}, s32[]{:S(2)}) async-start(s8[9961472]{0:T(1024)(128)(4,1)} %bitcast.525), calls=%async_computation.7 | async-start | bytes 3145728
  73.5 4.5 %copy-start.7 = (f32[16,16,512]{2,1,0:T(8,128)S(1)}, f32[16,16,512]{2,1,0:T(8,128)}, u32[]{:S(2)}) copy-start(f32[16,16,512]{2,1,0:T(8,128)} %get-tuple-element.9) | copy-start | bytes 1572868
  75.0 3.2 %copy-start.6 = (f32[16,16,512]{2,1,0:T(8,128)S(1)}, f32[16,16,512]{2,1,0:T(8,128)}, u32[]{:S(2)}) copy-start(f32[16,16,512]{2,1,0:T(8,128)} %get-tuple-element.8) | copy-start | bytes 1572868
  76.5 2.0 %copy-start.5 = (f32[16,16,512]{2,1,0:T(8,128)S(1)}, f32[16,16,512]{2,1,0:T(8,128)}, u32[]{:S(2)}) copy-start(f32[16,16,512]{2,1,0:T(8,128)} %get-tuple-element.7) | copy-start | bytes 1572868
  76.9 1.9 %copy-start.4 = (f32[16,16,512]{2,1,0:T(8,128)S(1)}, f32[16,16,512]{2,1,0:T(8,128)}, u32[]{:S(2)}) copy-start(f32[16,16,512]{2,1,0:T(8,128)} %get-tuple-element.6) | copy-start | bytes 1572868
  77.1 1.9 %copy-start.3 = (f32[16,16,512]{2,1,0:T(8,128)S(1)}, f32[16,16,512]{2,1,0:T(8,128)}, u32[]{:S(2)}) copy-start(f32[16,16,512]{2,1,0:T(8,128)} %get-tuple-element.5) | copy-start | bytes 1572868
  77.7 10.1 %copy-start.19 = (f32[64]{0:T(128)S(1)}, f32[64]{0:T(128)}, u32[]{:S(2)}) copy-start(f32[64]{0:T(128)} %param.9) | copy-start | bytes 772
  79.3 3.8 %copy-start.1 = (f32[19,16,16,512]{3,2,1,0:T(8,128)}, f32[19,16,16,512]{3,2,1,0:T(8,128)S(1)}, u32[]{:S(2)}) copy-start(f32[19,16,16,512]{3,2,1,0:T(8,128)S(1)} %bitcast_dynamic-update-slice_fusion) | copy-start | bytes 29884420
  84.4 10.0 %collective-permute-start.1 = (f32[19,1,16,512]{3,2,1,0:T(8,128)S(1)}, f32[19,1,16,512]{3,2,1,0:T(8,128)S(1)}, u32[]{:S(2)}, u32[]{:S(2)}) collective-permute-start(f32[19,1,16,512]{3,2,1,0:T(8,128)S(1)} %get-tuple-element.45), channel_id=1, source_target_pairs={{8,0},{16,8},{24,16},{32,24},{40,32},{48,40},{56,48},{64,56},{72,6... | collective-permute-start | bytes 1867784 | tf_op jit(solution)/shard_map/ppermute | solution.py:43
  86.6 11.8 %collective-permute-start = (f32[19,1,16,512]{3,2,1,0:T(8,128)S(1)}, f32[19,1,16,512]{3,2,1,0:T(8,128)S(1)}, u32[]{:S(2)}, u32[]{:S(2)}) collective-permute-start(f32[19,1,16,512]{3,2,1,0:T(8,128)S(1)} %get-tuple-element.46), channel_id=1, source_target_pairs={{0,8},{8,16},{16,24},{24,32},{32,40},{40,48},{48,56},{56,64},{64,7... | collective-permute-start | bytes 1867784 | tf_op jit(solution)/shard_map/ppermute | solution.py:41
  103.7 23.7 %collective-permute-start.3 = (f32[19,18,1,512]{3,2,1,0:T(1,128)}, f32[19,18,1,512]{3,2,1,0:T(1,128)S(1)}, u32[]{:S(2)}, u32[]{:S(2)}) collective-permute-start(f32[19,18,1,512]{3,2,1,0:T(1,128)} %get-tuple-element.39), channel_id=1, source_target_pairs={{1,0},{2,1},{3,2},{4,3},{5,4},{6,5},{7,6},{0,7},{9,8},{10,9},{11,1... | collective-permute-start | bytes 2101256 | tf_op jit(solution)/shard_map/ppermute | solution.py:43
  109.4 17.2 %collective-permute-start.2 = (f32[19,18,1,512]{3,2,1,0:T(1,128)}, f32[19,18,1,512]{3,2,1,0:T(1,128)S(1)}, u32[]{:S(2)}, u32[]{:S(2)}) collective-permute-start(f32[19,18,1,512]{3,2,1,0:T(1,128)} %get-tuple-element.40), channel_id=1, source_target_pairs={{0,1},{1,2},{2,3},{3,4},{4,5},{5,6},{6,7},{7,0},{8,9},{9,10},{10,1... | collective-permute-start | bytes 2101256 | tf_op jit(solution)/shard_map/ppermute | solution.py:41
  110.7 15.8 %slice-start = ((s8[9961472]{0:T(1024)(128)(4,1)}), s8[4194304]{0:T(1024)(128)(4,1)S(1)}, s32[]{:S(2)}) async-start(s8[9961472]{0:T(1024)(128)(4,1)} %bitcast.523), calls=%async_computation.2 | async-start | bytes 8388608
  110.7 15.8 %slice-start.1 = ((s8[9961472]{0:T(1024)(128)(4,1)}), s8[4194304]{0:T(1024)(128)(4,1)S(1)}, s32[]{:S(2)}) async-start(s8[9961472]{0:T(1024)(128)(4,1)} %bitcast.523), calls=%async_computation.3 | async-start | bytes 8388608
  112.8 13.8 %slice-start.2 = ((s8[9961472]{0:T(1024)(128)(4,1)}), s8[1572864]{0:T(1024)(128)(4,1)S(1)}, s32[]{:S(2)}) async-start(s8[9961472]{0:T(1024)(128)(4,1)} %bitcast.523), calls=%async_computation.4 | async-start | bytes 3145728
  115.4 14.0 %copy-start.2 = (f32[16,16,511]{2,1,0:T(8,128)S(1)}, f32[16,16,511]{2,1,0:T(8,128)}, u32[]{:S(2)}) copy-start(f32[16,16,511]{2,1,0:T(8,128)} %slice.347) | copy-start | bytes 1569796
where the time goes:
time: 144 us; the launch traced here: 143 us
  other arithmetic  60.8 us (42%)
  local copies, waits for them, and re-layouts  33.2 us (23%)
  waiting for transfers between devices  27.9 us (19%)
  starting transfers between devices  19.1 us (13%)
    unnamed x35, other arithmetic  33.4 us
    ppermute x2, waiting for transfers between devices, with_halo(): lax.ppermute(tail, axis, [(i, (i + 1) % count) for i in range(count)])  15.2 us
    mul x1, other arithmetic, per_device(): heat * heat_factor(tau_fine)  13.1 us
    unnamed x53, local copies, waits for them, and re-layouts  7.92 us
    ppermute x2, starting transfers between devices, with_halo(): lax.ppermute(head, axis, [((i + 1) % count, i) for i in range(count)])  7.92 us
    all_to_all x1, starting transfers between devices, per_device(): lax.all_to_all(tau_owner, 'gy', split_axis=1, concat_axis=2, tiled=True)  7.01 us
    reshape x1, local copies, waits for them, and re-layouts, block_mean(): field.reshape(a // 8, 8, b // 8, 8, c // 8, 8).sum(axis=(1, 3, 5)) / 512.0  6.99 us
    reshape x1, local copies, waits for them, and re-layouts, expand(): jnp.broadcast_to(coarse[:, None, :, None, :, None], (a, 8, b, 8, c, 8))  6.86 us
  transfers between devices with their start and end apart: 6, of which 4 were waited for; matrix products, arithmetic and copies ran while one was open for 22% of the time, Pallas kernels for 0%

commit v1 on v0

v1 whole, which is shorter than its diff:
```python
import functools

import jax
import jax.numpy as jnp
from jax import lax
from jax.experimental import pallas as pl
from jax.experimental.pallas import tpu as pltpu
from jax.sharding import PartitionSpec as P

SUB = 4
MESH = pl.DeviceIdType.MESH
F32 = jnp.float32
HIGH = lax.Precision.HIGHEST

velocities = (
    (0, 0, 0),
    (1, 0, 0),
    (-1, 0, 0),
    (0, 1, 0),
    (0, -1, 0),
    (0, 0, 1),
    (0, 0, -1),
    (1, 1, 0),
    (-1, -1, 0),
    (1, -1, 0),
    (-1, 1, 0),
    (1, 0, 1),
    (-1, 0, -1),
    (1, 0, -1),
    (-1, 0, 1),
    (0, 1, 1),
    (0, -1, -1),
    (0, 1, -1),
    (0, -1, 1),
)
opposite = (0, 2, 1, 4, 3, 6, 5, 8, 7, 10, 9, 12, 11, 14, 13, 16, 15, 18, 17)

LEAVE_X = ((1, 7, 9, 11, 13), (2, 8, 10, 12, 14))
LEAVE_Y = ((3, 7, 10, 15, 17), (4, 8, 9, 16, 18))
LEAVE_Z = (5, 6, 11, 12, 13, 14, 15, 16, 17, 18)
CORNERS = ((7, 0, 1), (10, 0, -1), (9, 1, 1), (8, 1, -1))
TILES = tuple(slice(128 * t, 128 * t + 128) for t in range(4))


def iota(shape, axis):
    return lax.broadcasted_iota(jnp.int32, shape, axis)


def class_load(counts, lanes):
    volume = (iota((64, lanes), 0).astype(F32) + 1.0) / 64.0
    return jnp.dot(counts, volume, precision=HIGH, preferred_element_type=F32)


def relax_time(load):
    packed = 0.5 * load / (1.0 + load)
    thinned = 1.0 - packed / 0.64
    return 0.5 + 3.0 * (0.04 / (thinned * thinned))


def moments_of(f):
    even = {i: f[i] + f[i + 1] for i in range(1, 19, 2)}
    odd = {i: f[i] - f[i + 1] for i in range(1, 19, 2)}
    xy, xz, yz = even[7] + even[9], even[11] + even[13], even[15] + even[17]
    rho = f[0] + (even[1] + xy) + (even[3] + yz) + (even[5] + xz)
    jx = odd[1] + (odd[7] + odd[9]) + (odd[11] + odd[13])
    jy = odd[3] + (odd[7] - odd[9]) + (odd[15] + odd[17])
    jz = odd[5] + (odd[11] - odd[13]) + (odd[15] - odd[17])
    return even, (xy, xz, yz), rho, (jx, jy, jz)


def equilibrium(eighth, ux, uy, uz):
    tx, ty, tz = eighth * ux, eighth * uy, eighth * uz
    xx, yy, zz = tx * ux, ty * uy, tz * uz
    tx2, ty2 = tx + tx, ty + ty
    cross = (tx2 * uy, tx2 * uz, ty2 * uz)
    base = eighth * (8.0 / 36.0) - (xx + yy + zz) * (1.0 / 3.0)
    bx, by, bz = base + xx, base + yy, base + zz
    sums = (bx + yy, bx + zz, by + zz)
    return base, (bx, by, bz), sums, cross, (tx * (2.0 / 3.0), ty * (2.0 / 3.0), tz * (2.0 / 3.0))


def equilibrium_of(index, terms):
    base, axes, sums, cross, flow = terms
    c = velocities[index]
    nonzero = [a for a in range(3) if c[a] != 0]
    if not nonzero:
        return 12.0 * base
    if len(nonzero) == 1:
        (a,) = nonzero
        even = axes[a] + axes[a]
        odd = flow[a] + flow[a]
        return even + odd if c[a] > 0 else even - odd
    a, b = nonzero
    slot = {(0, 1): 0, (0, 2): 1, (1, 2): 2}[(a, b)]
    even = sums[slot] + cross[slot] if c[a] * c[b] > 0 else sums[slot] - cross[slot]
    odd = flow[a] + flow[b] if c[a] == c[b] else flow[a] - flow[b]
    return even + odd if c[a] > 0 else even - odd


def along_lanes(tiles, step):
    if step == 0:
        return tiles
    lane = iota((8, 128), 1)
    if step > 0:
        moved = [pltpu.roll(v, 1, 1) for v in tiles]
        return [jnp.where(lane == 0, moved[(t + 3) % 4], moved[t]) for t in range(4)]
    moved = [pltpu.roll(v, 127, 1) for v in tiles]
    return [jnp.where(lane == 127, moved[(t + 1) % 4], moved[t]) for t in range(4)]


def along_rows(low, high, step):
    if step == 0:
        return low, high
    row = iota((8, 128), 0)
    if step > 0:
        low, high = pltpu.roll(low, 1, 0), pltpu.roll(high, 1, 0)
        return jnp.where(row == 0, high, low), jnp.where(row == 0, low, high)
    low, high = pltpu.roll(low, 7, 0), pltpu.roll(high, 7, 0)
    return jnp.where(row == 7, high, low), jnp.where(row == 7, low, high)


def step_kernel(
    nx,
    ny,
    pop_hbm,
    solid_hbm,
    counts_hbm,
    moved,
    sums_in,
    pops,
    solid,
    counts,
    moments,
    heat_acc,
    sums_out,
    rate_out,
    rate_in,
    rates,
    staged,
    row_pops,
    row_solid,
    start_out,
    gain_out,
    edge_out,
    corner_in,
    corner_own,
    pop_sem,
    solid_sem,
    counts_sem,
    row_sem,
    rate_send,
    rate_recv,
    sums_send,
    sums_recv,
    edge_send,
    edge_recv,
    corner_send,
    corner_recv,
    onward_send,
    onward_recv,
):
    gx = lax.axis_index("gx")
    gy = lax.axis_index("gy")
    right, left = lax.rem(gx + 1, nx), lax.rem(gx + nx - 1, nx)
    up, down = lax.rem(gy + 1, ny), lax.rem(gy + ny - 1, ny)
    peers = [lax.rem(gy + d, ny) for d in range(ny)]

    counts_copy = pltpu.make_async_copy(counts_hbm, counts, counts_sem)
    counts_copy.start()
    barrier = pltpu.get_barrier_semaphore()
    partners = [(gx, peers[d]) for d in range(1, ny)] + [(left, gy), (right, gy)]
    for partner in partners:
        pl.semaphore_signal(barrier, inc=1, device_id=partner, device_id_type=MESH)

    def chunk_copy(chunk):
        rows = pl.ds(2 * chunk, 2)
        return pltpu.make_async_copy(pop_hbm.at[:, rows], pops.at[:, rows], pop_sem.at[chunk])

    def row_copies(side):
        y = 15 if side == 0 else 0
        return (
            pltpu.make_async_copy(solid_hbm.at[:, y], row_solid.at[side], row_sem.at[side, 0]),
            pltpu.make_async_copy(pop_hbm.at[:, :, y], row_pops.at[side], row_sem.at[side, 1]),
        )

    solid_copy = pltpu.make_async_copy(solid_hbm, solid, solid_sem)
    for side in range(2):
        for copy in row_copies(side):
            copy.start()
    solid_copy.start()
    for chunk in (0, 7, 1, 2, 3, 4, 5, 6):
        chunk_copy(chunk).start()

    counts_copy.wait()
    row, lane = iota((256, 128), 0), iota((256, 128), 1)
    load = class_load(counts[...], 128)
    load = jnp.where(row % 8 == (lane % 64) // 8, load, 0.0)
    slot, cell = iota((64, 256), 0), iota((64, 256), 1)
    wanted = ((slot % 8) // 2) * 16 + 2 * (slot // 8) + slot % 2
    pick = jnp.where((slot % 8 < 4) & (cell // 8 == wanted), 1.0, 0.0)
    load = jnp.dot(pick, load, precision=HIGH, preferred_element_type=F32)
    rate_out[...] = (1.0 / relax_time(load)).reshape(8, 8, 128)
    rate_in[pl.ds(gy, 1)] = rate_out[pl.ds(gy, 1)]

    pl.semaphore_wait(barrier, len(partners))

    def rate_copy(d):
        return pltpu.make_async_remote_copy(
            src_ref=rate_out.at[peers[d]],
            dst_ref=rate_in.at[gy],
            send_sem=rate_send.at[d],
            recv_sem=rate_recv.at[d],
            device_id=(gx, peers[d]),
            device_id_type=MESH,
        )

    for d in range(1, ny):
        rate_copy(d).start()

    heat_acc[...] = jnp.zeros_like(heat_acc)
    sums_out[...] = jnp.zeros_like(sums_out)

    def prepare(kind, side, tile):
        lanes = pl.ds(pl.multiple_of(tile * 128, 128), 128)
        leave = (LEAVE_X if kind == 0 else LEAVE_Y)[side]
        plane = 15 if side == 0 else 0
        for part in range(2):
            rows = slice(8 * part, 8 * part + 8)
            if kind == 0:
                f = [pops[index, plane, rows, lanes] for index in range(19)]
                fluid = solid[plane, rows, lanes] == 0
            else:
                f = [row_pops[side, index, rows, lanes] for index in range(19)]
                fluid = row_solid[side, rows, lanes] == 0
            _, _, rho, (jx, jy, jz) = moments_of(f)
            inverse = 1.0 / rho
            terms = equilibrium(rho * 0.125, jx * inverse, jy * inverse, jz * inverse)
            for place, index in enumerate(leave):
                start_out[kind, side, place, rows, lanes] = jnp.where(
                    fluid, f[index], f[opposite[index]]
                )
                gain_out[kind, side, place, rows, lanes] = jnp.where(
                    fluid, equilibrium_of(index, terms) - f[index], 0.0
                )

    for side in range(2):
        for copy in row_copies(side):
            copy.wait()

    def prepare_y(tile, carry):
        for side in range(2):
            prepare(1, side, tile)
        return carry

    lax.fori_loop(0, 4, prepare_y, 0)

    solid_copy.wait()
    for chunk in (0, 7):
        chunk_copy(chunk).wait()

    def prepare_x(tile, carry):
        for side in range(2):
            prepare(0, side, tile)
        return carry

    lax.fori_loop(0, 4, prepare_x, 0)

    def first_pass(chunk):
        half = chunk // 4

        def one_tile(tile, carry):
            lanes = pl.ds(pl.multiple_of(tile * 128, 128), 128)
            heats = []
            for part in range(4):
                plane, rows = 2 * chunk + part // 2, slice(8 * (part % 2), 8 * (part % 2) + 8)
                f = [pops[index, plane, rows, lanes] for index in range(19)]
                even, (xy, xz, yz), rho, (jx, jy, jz) = moments_of(f)
                inverse = 1.0 / rho
                ux, uy, uz = jx * inverse, jy * inverse, jz * inverse
                third = rho * (1.0 / 3.0)
                pxx = even[1] + (xy + xz) - third - jx * ux
                pyy = even[3] + (xy + yz) - third - jy * uy
                pzz = even[5] + (xz + yz) - third - jz * uz
                pxy = even[7] - even[9] - jx * uy
                pxz = even[11] - even[13] - jx * uz
                pyz = even[15] - even[17] - jy * uz
                off = pxy * pxy + pxz * pxz + pyz * pyz
                square = pxx * pxx + pyy * pyy + pzz * pzz + (off + off)
                heat = square * (inverse * inverse)
                heats.append(jnp.where(solid[plane, rows, lanes] == 0, heat, 0.0))
                for slot, value in enumerate((rho, ux, uy, uz)):
                    moments[slot, plane, rows, lanes] = value
            heat_acc[half * 2, tile] += heats[0] + heats[2]
            heat_acc[half * 2 + 1, tile] += heats[1] + heats[3]
            return carry

        lax.fori_loop(0, 4, one_tile, 0)

    def outer_chunks(step, carry):
        first_pass(step * 7)
        return carry

    def inner_chunks(chunk, carry):
        chunk_copy(chunk).wait()
        first_pass(chunk)
        return carry

    lax.fori_loop(0, 2, outer_chunks, 0)
    lax.fori_loop(1, 7, inner_chunks, 0)

    for d in range(1, ny):
        rate_copy(d).wait_recv()
    lane = iota((8, 128), 1)
    for tile in range(4):
        owned = jnp.where(lane < 64, rate_in[2 * tile], rate_in[2 * tile + 1])
        for block in range(4):
            rates[block, tile] = jnp.broadcast_to(owned[block : block + 1], (8, 128))

    def edge_copy(kind, side, place):
        index = (LEAVE_X if kind == 0 else LEAVE_Y)[side][place]
        source = edge_out.at[kind, side, place]
        if kind == 0:
            target = moved.at[index, 1 if side == 0 else 16]
            device = (right if side == 0 else left, gy)
        else:
            first = 1 + velocities[index][0]
            target = moved.at[index, first : first + 16, 0 if side == 0 else 15]
            device = (gx, up if side == 0 else down)
        return pltpu.make_async_remote_copy(
            src_ref=source,
            dst_ref=target,
            send_sem=edge_send.at[kind, side, place],
            recv_sem=edge_recv.at[kind, side, place],
            device_id=device,
            device_id_type=MESH,
        )

    def corner_copy(slot):
        index, side, step = CORNERS[slot]
        return pltpu.make_async_remote_copy(
            src_ref=edge_out.at[1, side, LEAVE_Y[side].index(index), 15 if step > 0 else 0],
            dst_ref=corner_in.at[slot, 0],
            send_sem=corner_send.at[slot],
            recv_sem=corner_recv.at[slot],
            device_id=(right if step > 0 else left, gy),
            device_id_type=MESH,
        )

    def onward_copy(slot):
        _, side, _ = CORNERS[slot]
        return pltpu.make_async_remote_copy(
            src_ref=corner_in.at[slot, 0],
            dst_ref=corner_own.at[slot, 0],
            send_sem=onward_send.at[slot],
            recv_sem=onward_recv.at[slot],
            device_id=(gx, up if side == 0 else down),
            device_id_type=MESH,
        )

    def leave(kind, side):
        for place, index in enumerate((LEAVE_X if kind == 0 else LEAVE_Y)[side]):
            c = velocities[index]
            values = []
            for part in range(2):
                rows = slice(8 * part, 8 * part + 8)
                far = 1 - side
                blocks = far * 2 + part if kind == 0 else part * 2 + far
                tiles = [
                    start_out[kind, side, place, rows, TILES[t]]
                    + rates[blocks, t] * gain_out[kind, side, place, rows, TILES[t]]
                    for t in range(4)
                ]
                values.append(along_lanes(tiles, c[2]))
            for t in range(4):
                low, high = along_rows(values[0][t], values[1][t], c[1] if kind == 0 else 0)
                edge_out[kind, side, place, 0:8, TILES[t]] = low
                edge_out[kind, side, place, 8:16, TILES[t]] = high
            edge_copy(kind, side, place).start()

    for kind in (1, 0):
        for side in range(2):
            leave(kind, side)
    for slot in range(4):
        corner_copy(slot).start()

    for tile in range(4):
        sums_out[tile, 0:4, :] = jnp.sum(heat_acc[:, tile], axis=1)
    sums_in[pl.ds(gy, 1)] = sums_out[pl.ds(gy // 2, 1)]

    def sums_copy(d):
        return pltpu.make_async_remote_copy(
            src_ref=sums_out.at[peers[d] // 2],
            dst_ref=sums_in.at[gy],
            send_sem=sums_send.at[d],
            recv_sem=sums_recv.at[d],
            device_id=(gx, peers[d]),
            device_id_type=MESH,
        )

    for d in range(1, ny):
        sums_copy(d).start()

    def put(index, plane, tile, low, high):
        c = velocities[index]
        place, lanes = plane + 1 + c[0], TILES[tile]
        low, high = along_rows(low, high, c[1])
        if c[1] > 0:
            moved[index, place, 1:8, lanes] = low[1:8]
        else:
            moved[index, place, 0:8, lanes] = low
        if c[1] < 0:
            moved[index, place, 8:15, lanes] = high[0:7]
        else:
            moved[index, place, 8:16, lanes] = high

    def collide(plane):
        half = plane // 8
        for tile in range(4):
            lanes = TILES[tile]
            found = []
            for part in range(2):
                rows = slice(8 * part, 8 * part + 8)
                rho, ux, uy, uz = [moments[slot, plane, rows, lanes] for slot in range(4)]
                rate = rates[half * 2 + part, tile]
                terms = equilibrium((rate * 0.125) * rho, ux, uy, uz)
                fluid = solid[plane, rows, lanes] == 0
                kept = 1.0 - rate
                f = [pops[index, plane, rows, lanes] for index in range(19)]
                found.append(
                    [
                        jnp.where(
                            fluid, kept * f[index] + equilibrium_of(index, terms), f[opposite[index]]
                        )
                        for index in range(19)
                    ]
                )
            for index in range(19):
                low, high = found[0][index], found[1][index]
                if index in LEAVE_Z:
                    staged[LEAVE_Z.index(index), 0:8, lanes] = low
                    staged[LEAVE_Z.index(index), 8:16, lanes] = high
                else:
                    put(index, plane, tile, low, high)

    def run_z(plane):
        for place, index in enumerate(LEAVE_Z):
            low = along_lanes([staged[place, 0:8, TILES[t]] for t in range(4)], velocities[index][2])
            high = along_lanes([staged[place, 8:16, TILES[t]] for t in range(4)], velocities[index][2])
            for t in range(4):
                put(index, plane, t, low[t], high[t])

    collide(0)

    def planes(plane, carry):
        run_z(plane - 1)
        collide(plane)
        return carry

    lax.fori_loop(1, 16, planes, 0)
    run_z(15)

    for slot in range(4):
        corner_copy(slot).wait_recv()
        onward_copy(slot).start()

    for kind in range(2):
        for side in range(2):
            for place in range(5):
                edge_copy(kind, side, place).wait_recv()
    for slot, (index, side, step) in enumerate(CORNERS):
        onward_copy(slot).wait_recv()
        row = 0 if side == 0 else 15
        moved[index, 1 if step > 0 else 16, row : row + 1, :] = corner_own[slot, 0:1, :]
    for d in range(1, ny):
        sums_copy(d).wait_recv()

    for d in range(1, ny):
        rate_copy(d).wait_send()
        sums_copy(d).wait_send()
    for kind in range(2):
        for side in range(2):
            for place in range(5):
                edge_copy(kind, side, place).wait_send()
    for slot in range(4):
        corner_copy(slot).wait_send()
        onward_copy(slot).wait_send()


def finish_kernel(
    moved,
    sums_in,
    counts_hbm,
    breakage_hbm,
    selection_hbm,
    read_hbm,
    next_hbm,
    counts,
    breakage,
    selection,
    result,
    small_sem,
    read_sem,
    next_sem,
):
    copies = [
        pltpu.make_async_copy(moved.at[index, 1:17], read_hbm.at[index], read_sem.at[index])
        for index in range(19)
    ]
    loads = [
        pltpu.make_async_copy(counts_hbm, counts, small_sem.at[0]),
        pltpu.make_async_copy(breakage_hbm, breakage, small_sem.at[1]),
        pltpu.make_async_copy(selection_hbm, selection, small_sem.at[2]),
    ]
    for copy in loads + copies:
        copy.start()
    for copy in loads:
        copy.wait()

    gy = lax.axis_index("gy")
    current = counts[...]
    tau = relax_time(class_load(current, 128))
    factor = (tau - 0.5) / (3.0 * tau * tau)
    row, slot = iota((256, 64), 0), iota((256, 64), 1)
    wanted = ((row // 8) % 16 // 2) * 8 + (row // 128) * 2 + (row // 8) % 2
    pick = jnp.where(slot == wanted, 1.0, 0.0)
    sums = jnp.dot(
        pick, sums_in[...].reshape(64, 128), precision=HIGH, preferred_element_type=F32
    )
    row, lane = iota((256, 128), 0), iota((256, 128), 1)
    sums = jnp.where(lane // 8 == row % 8 + 8 * lax.rem(gy, 2), sums, 0.0)
    sums = jnp.dot(sums, jnp.ones((128, 128), F32), precision=HIGH, preferred_element_type=F32)
    eps = sums * (4.5 / 512.0) * factor
    strength = jnp.sqrt(50.0 * eps + 1e-06)
    gain = strength / (1.0 + strength)
    rate = gain[:, :64] * selection[...][None, :]
    for step in range(SUB):
        lost = rate * current
        born = lax.dot_general(
            lost,
            breakage[...],
            (((1,), (1,)), ((), ())),
            precision=HIGH,
            preferred_element_type=F32,
        )
        current = current + 0.25 * (born - lost)
    result[...] = current
    last = pltpu.make_async_copy(result, next_hbm, next_sem)
    last.start()
    last.wait()
    for copy in copies:
        copy.wait()


def per_device(nx, ny, populations, solid, counts, breakage, selection):
    cells = counts.transpose(1, 2, 3, 0).reshape(256, 64)
    any_space = pl.BlockSpec(memory_space=pl.ANY)
    vmem = pl.BlockSpec(memory_space=pltpu.VMEM)
    dma = pltpu.SemaphoreType.DMA
    moved, sums = pl.pallas_call(
        functools.partial(step_kernel, nx, ny),
        out_shape=(
            pltpu.VMEM((19, 18, 16, 512), F32),
            pltpu.VMEM((8, 8, 128), F32),
        ),
        in_specs=[any_space] * 3,
        out_specs=(vmem, vmem),
        scratch_shapes=[
            pltpu.VMEM((19, 16, 16, 512), F32),
            pltpu.VMEM((16, 16, 512), jnp.int32),
            pltpu.VMEM((256, 64), F32),
            pltpu.VMEM((4, 16, 16, 512), F32),
            pltpu.VMEM((4, 4, 8, 128), F32),
            pltpu.VMEM((4, 8, 128), F32),
            pltpu.VMEM((8, 8, 128), F32),
            pltpu.VMEM((8, 8, 128), F32),
            pltpu.VMEM((4, 4, 8, 128), F32),
            pltpu.VMEM((10, 16, 512), F32),
            pltpu.VMEM((2, 19, 16, 512), F32),
            pltpu.VMEM((2, 16, 512), jnp.int32),
            pltpu.VMEM((2, 2, 5, 16, 512), F32),
            pltpu.VMEM((2, 2, 5, 16, 512), F32),
            pltpu.VMEM((2, 2, 5, 16, 512), F32),
            pltpu.VMEM((4, 8, 512), F32),
            pltpu.VMEM((4, 8, 512), F32),
            dma((8,)),
            dma,
            dma,
            dma((2, 2)),
            dma((8,)),
            dma((8,)),
            dma((8,)),
            dma((8,)),
            dma((2, 2, 5)),
            dma((2, 2, 5)),
            dma((4,)),
            dma((4,)),
            dma((4,)),
            dma((4,)),
        ],
        compiler_params=pltpu.CompilerParams(
            collective_id=0, has_side_effects=True, vmem_limit_bytes=40 * 1024 * 1024
        ),
        name="collide",
    )(*[pltpu.with_memory_space_constraint(x, pltpu.HBM) for x in (populations, solid, cells)])
    read, after = pl.pallas_call(
        finish_kernel,
        out_shape=(
            jax.ShapeDtypeStruct(populations.shape, F32),
            jax.ShapeDtypeStruct(cells.shape, F32),
        ),
        in_specs=[vmem] * 2 + [any_space] * 3,
        out_specs=(any_space, any_space),
        scratch_shapes=[
            pltpu.VMEM((256, 64), F32),
            pltpu.VMEM((64, 64), F32),
            pltpu.VMEM((64,), F32),
            pltpu.VMEM((256, 64), F32),
            dma((3,)),
            dma((19,)),
            dma,
        ],
        compiler_params=pltpu.CompilerParams(vmem_limit_bytes=24 * 1024 * 1024),
        name="finish",
    )(moved, sums, cells, breakage, selection)
    return (read, after.reshape(2, 16, 8, 64).transpose(3, 0, 1, 2))


def solution(mesh):
    in_specs = (P(None, "gx", "gy", None), P("gx", "gy", None), P(None, "gx", None, "gy"), P(), P())
    out_specs = (P(None, "gx", "gy", None), P(None, "gx", None, "gy"))
    return jax.shard_map(
        functools.partial(per_device, mesh.shape["gx"], mesh.shape["gy"]),
        mesh=mesh,
        in_specs=in_specs,
        out_specs=out_specs,
        check_vma=False,
    )
```

time: 144 us -> 31.3 us (0.22)
  other arithmetic: 60.8 us -> 0 us
  local copies, waits for them, and re-layouts: 33.2 us -> 0.01 us
  Pallas kernels: 0 us -> 30.5 us
  waiting for transfers between devices: 27.9 us -> 0 us
  starting transfers between devices: 19.1 us -> 0 us
    unnamed x35 -> x0, other arithmetic: 33.4 us -> none
    pallas_call x0 -> x2, Pallas kernels: none -> 30.5 us  [the longest x1 26.3 us: per_device(): pl.pallas_call(functools.partial(step_kernel, nx, ny), out_shape=(pltpu.V...]
    ppermute x4 -> x0, waiting for transfers between devices: 21.2 us -> none  [the longest x2 15.2 us: with_halo(): lax.ppermute(tail, axis, [(i, (i + 1) % count) for i in range(count)])]
    reshape x3 -> x0, local copies, waits for them, and re-layouts: 14.8 us -> none  [the longest x1 6.99 us: block_mean(): field.reshape(a // 8, 8, b // 8, 8, c // 8, 8).sum(axis=(1, 3, 5)) / 512.0]
    mul x1 -> x0, other arithmetic: 13.1 us -> none  [per_device(): heat * heat_factor(tau_fine)]
    all_to_all x2 -> x0, starting transfers between devices: 11.2 us -> none  [the longest x1 7.01 us: per_device(): lax.all_to_all(tau_owner, 'gy', split_axis=1, concat_axis=2, tiled=True)]
    ppermute x4 -> x0, starting transfers between devices: 7.92 us -> none  [the longest x2 7.92 us: with_halo(): lax.ppermute(head, axis, [((i + 1) % count, i) for i in range(count)])]
    unnamed x53 -> x6, local copies, waits for them, and re-layouts: 7.92 us -> 0.01 us
  transfers between devices with their start and end apart: 6 -> 0, of which waited for: 4 -> 0; matrix products, arithmetic and copies ran while one was open for 22% -> 0% of each run, Pallas kernels for 0% -> 0%
where the time goes in v1:
time: 31.3 us; the launch traced here: 31.2 us
  Pallas kernels  30.5 us (97%)
  between operations  0.69 us (2%)
    pallas_call x1, Pallas kernels, per_device(): pl.pallas_call(functools.partial(step_kernel, nx, ny), out_shape=(pltpu.V...  26.3 us
    pallas_call x1, Pallas kernels, per_device(): pl.pallas_call(finish_kernel, out_shape=(jax.ShapeDtypeStruct(populations...  4.21 us

profile of v1, /device:TPU:0, one launch (start us, length us, event | category | flops | bytes accessed | tf_op | source)
XLA Modules:
  0.0 31.2 jit_solution(12583053543623048833)
XLA Ops:
  0.6 0.0 copy-start.2
  0.6 0.0 copy-start.1
  0.7 0.0 copy-start
  0.7 26.3 %collide.1 = (f32[19,18,16,512]{3,2,1,0:T(8,128)S(1)}, f32[8,8,128]{2,1,0:T(8,128)S(1)}) custom-call(f32[19,16,16,512]{3,2,1,0:T(8,128)} %pop_hbm.1, s32[16,16,512]{2,1,0:T(8,128)} %solid_hbm.1, f32[256,64]{1,0:T(8,128)} %bitcast.6), custom_call_target="tpu_custom_call" | custom-call | tf_op jit(solution)/shard_map/collide/pallas_call | solution.py:559
  26.9 0.0 copy-done.2
  27.0 0.0 copy-done.1
  27.0 0.0 copy-done
  27.0 4.2 %finish.1 = (f32[19,16,16,512]{3,2,1,0:T(8,128)}, f32[256,64]{1,0:T(8,128)}) custom-call(f32[19,18,16,512]{3,2,1,0:T(8,128)S(1)} %get-tuple-element.6.moved, f32[8,8,128]{2,1,0:T(8,128)S(1)} %get-tuple-element.7.sums_in, f32[256,64]{1,0:T(8,128)S(1)} %bitcast.7, f32[64,64]{1,0:T(8,128)S(1)} %copy-done.1, f32[64]{0:T(128)S(1)} %copy-done.2), custom_call_target="tpu_custom_call" | custom-call | tf_op jit(solution)/shard_map/finish/pallas_call | solution.py:605
Async XLA Ops:
  0.6 26.3 %copy-start.2 = (f32[64]{0:T(128)S(1)}, f32[64]{0:T(128)}, u32[]{:S(2)}) copy-start(f32[64]{0:T(128)} %selection_hbm.1) | copy-start | bytes 772
  0.6 26.3 %copy-start.1 = (f32[64,64]{1,0:T(8,128)S(1)}, f32[64,64]{1,0:T(8,128)}, u32[]{:S(2)}) copy-start(f32[64,64]{1,0:T(8,128)} %breakage_hbm.1) | copy-start | bytes 49156
  0.7 26.3 %copy-start = (f32[64,2,16,8]{0,3,2,1:T(8,128)S(1)}, f32[64,2,16,8]{0,3,2,1:T(8,128)}, u32[]{:S(2)}) copy-start(f32[64,2,16,8]{0,3,2,1:T(8,128)} %param.7) | copy-start | bytes 196612

commit v2 on v1

--- a/solution.py
+++ b/solution.py
@@ -188,7 +188,7 @@
         for copy in row_copies(side):
             copy.start()
     solid_copy.start()
-    for chunk in (0, 7, 1, 2, 3, 4, 5, 6):
+    for chunk in (0, 7, 1, 2):
         chunk_copy(chunk).start()
 
     counts_copy.wait()
@@ -302,6 +302,11 @@
 
     def inner_chunks(chunk, carry):
         chunk_copy(chunk).wait()
+
+        @pl.when(chunk < 5)
+        def _():
+            chunk_copy(chunk + 2).start()
+
         first_pass(chunk)
         return carry
 
@@ -357,31 +362,37 @@
             device_id_type=MESH,
         )
 
-    def leave(kind, side):
-        for place, index in enumerate((LEAVE_X if kind == 0 else LEAVE_Y)[side]):
-            c = velocities[index]
-            values = []
-            for part in range(2):
-                rows = slice(8 * part, 8 * part + 8)
-                far = 1 - side
-                blocks = far * 2 + part if kind == 0 else part * 2 + far
-                tiles = [
-                    start_out[kind, side, place, rows, TILES[t]]
-                    + rates[blocks, t] * gain_out[kind, side, place, rows, TILES[t]]
-                    for t in range(4)
-                ]
-                values.append(along_lanes(tiles, c[2]))
-            for t in range(4):
-                low, high = along_rows(values[0][t], values[1][t], c[1] if kind == 0 else 0)
-                edge_out[kind, side, place, 0:8, TILES[t]] = low
-                edge_out[kind, side, place, 8:16, TILES[t]] = high
-            edge_copy(kind, side, place).start()
-
-    for kind in (1, 0):
+    def leave(kind, side, place):
+        index = (LEAVE_X if kind == 0 else LEAVE_Y)[side][place]
+        c = velocities[index]
+        values = []
+        for part in range(2):
+            rows = slice(8 * part, 8 * part + 8)
+            far = 1 - side
+            blocks = far * 2 + part if kind == 0 else part * 2 + far
+            tiles = [
+                start_out[kind, side, place, rows, TILES[t]]
+                + rates[blocks, t] * gain_out[kind, side, place, rows, TILES[t]]
+                for t in range(4)
+            ]
+            values.append(along_lanes(tiles, c[2]))
+        for t in range(4):
+            low, high = along_rows(values[0][t], values[1][t], c[1] if kind == 0 else 0)
+            edge_out[kind, side, place, 0:8, TILES[t]] = low
+            edge_out[kind, side, place, 8:16, TILES[t]] = high
+
+    for slot, (index, side, _) in enumerate(CORNERS):
+        leave(1, side, LEAVE_Y[side].index(index))
+        corner_copy(slot).start()
+    for place in range(5):
         for side in range(2):
-            leave(kind, side)
-    for slot in range(4):
-        corner_copy(slot).start()
+            leave(0, side, place)
+            edge_copy(0, side, place).start()
+    for place in (1, 2, 0, 3, 4):
+        for side in range(2):
+            if (LEAVE_Y[side][place], side) not in [corner[:2] for corner in CORNERS]:
+                leave(1, side, place)
+            edge_copy(1, side, place).start()
 
     for tile in range(4):
         sums_out[tile, 0:4, :] = jnp.sum(heat_acc[:, tile], axis=1)
@@ -456,12 +467,19 @@
         collide(plane)
         return carry
 
-    lax.fori_loop(1, 16, planes, 0)
+    def some_planes(half, carry):
+        lax.fori_loop(1 + 8 * half, 9 + 7 * half, planes, 0)
+
+        @pl.when(half == 0)
+        def _():
+            for slot in range(4):
+                corner_copy(slot).wait_recv()
+                onward_copy(slot).start()
+
+        return carry
+
+    lax.fori_loop(0, 2, some_planes, 0)
     run_z(15)
-
-    for slot in range(4):
-        corner_copy(slot).wait_recv()
-        onward_copy(slot).start()
 
     for kind in range(2):
         for side in range(2):
@@ -511,7 +529,7 @@
         pltpu.make_async_copy(breakage_hbm, breakage, small_sem.at[1]),
         pltpu.make_async_copy(selection_hbm, selection, small_sem.at[2]),
     ]
-    for copy in loads + copies:
+    for copy in copies + loads:
         copy.start()
     for copy in loads:
         copy.wait()

time: 31.3 us -> 26.6 us (0.85)
  Pallas kernels: 30.5 us -> 25.7 us
    pallas_call x1, Pallas kernels: 26.3 us -> 21.7 us  [per_device(): pl.pallas_call(functools.partial(step_kernel, nx, ny), out_shape=(pltpu.V...]
where the time goes in v2:
time: 26.6 us; the launch traced here: 26.4 us
  Pallas kernels  25.7 us (97%)
  between operations  0.69 us (3%)
    pallas_call x1, Pallas kernels, per_device(): pl.pallas_call(functools.partial(step_kernel, nx, ny), out_shape=(pltpu.V...  21.7 us
    pallas_call x1, Pallas kernels, per_device(): pl.pallas_call(finish_kernel, out_shape=(jax.ShapeDtypeStruct(populations...  4 us

profile of v2, /device:TPU:0, one launch (start us, length us, event | category | flops | bytes accessed | tf_op | source)
XLA Modules:
  0.0 26.4 jit_solution(16972214541859091770)
XLA Ops:
  0.6 0.0 copy-start.2
  0.6 0.0 copy-start.1
  0.7 0.0 copy-start
  0.7 21.7 %collide.1 = (f32[19,18,16,512]{3,2,1,0:T(8,128)S(1)}, f32[8,8,128]{2,1,0:T(8,128)S(1)}) custom-call(f32[19,16,16,512]{3,2,1,0:T(8,128)} %pop_hbm.1, s32[16,16,512]{2,1,0:T(8,128)} %solid_hbm.1, f32[256,64]{1,0:T(8,128)} %bitcast.6), custom_call_target="tpu_custom_call" | custom-call | tf_op jit(solution)/shard_map/collide/pallas_call | solution.py:577
  22.4 0.0 copy-done.2
  22.4 0.0 copy-done.1
  22.4 0.0 copy-done
  22.4 4.0 %finish.1 = (f32[19,16,16,512]{3,2,1,0:T(8,128)}, f32[256,64]{1,0:T(8,128)}) custom-call(f32[19,18,16,512]{3,2,1,0:T(8,128)S(1)} %get-tuple-element.6.moved, f32[8,8,128]{2,1,0:T(8,128)S(1)} %get-tuple-element.7.sums_in, f32[256,64]{1,0:T(8,128)S(1)} %bitcast.7, f32[64,64]{1,0:T(8,128)S(1)} %copy-done.1, f32[64]{0:T(128)S(1)} %copy-done.2), custom_call_target="tpu_custom_call" | custom-call | tf_op jit(solution)/shard_map/finish/pallas_call | solution.py:623
Async XLA Ops:
  0.6 21.8 %copy-start.2 = (f32[64]{0:T(128)S(1)}, f32[64]{0:T(128)}, u32[]{:S(2)}) copy-start(f32[64]{0:T(128)} %selection_hbm.1) | copy-start | bytes 772
  0.6 21.8 %copy-start.1 = (f32[64,64]{1,0:T(8,128)S(1)}, f32[64,64]{1,0:T(8,128)}, u32[]{:S(2)}) copy-start(f32[64,64]{1,0:T(8,128)} %breakage_hbm.1) | copy-start | bytes 49156
  0.7 21.8 %copy-start = (f32[64,2,16,8]{0,3,2,1:T(8,128)S(1)}, f32[64,2,16,8]{0,3,2,1:T(8,128)}, u32[]{:S(2)}) copy-start(f32[64,2,16,8]{0,3,2,1:T(8,128)} %param.7) | copy-start | bytes 196612

commit v3 on v2

--- a/solution.py
+++ b/solution.py
@@ -38,7 +38,8 @@
 LEAVE_X = ((1, 7, 9, 11, 13), (2, 8, 10, 12, 14))
 LEAVE_Y = ((3, 7, 10, 15, 17), (4, 8, 9, 16, 18))
 LEAVE_Z = (5, 6, 11, 12, 13, 14, 15, 16, 17, 18)
-CORNERS = ((7, 0, 1), (10, 0, -1), (9, 1, 1), (8, 1, -1))
+CORNERS = ((7, 1, 1), (10, -1, 1), (9, 1, -1), (8, -1, -1))
+FLAT = tuple(i for i in range(19) if velocities[i][1] == 0)
 TILES = tuple(slice(128 * t, 128 * t + 128) for t in range(4))
 
 
@@ -126,6 +127,7 @@
     solid_hbm,
     counts_hbm,
     moved,
+    y_rows,
     sums_in,
     pops,
     solid,
@@ -142,8 +144,9 @@
     start_out,
     gain_out,
     edge_out,
+    y_out,
+    y_in,
     corner_in,
-    corner_own,
     pop_sem,
     solid_sem,
     counts_sem,
@@ -154,10 +157,10 @@
     sums_recv,
     edge_send,
     edge_recv,
+    y_send,
+    y_recv,
     corner_send,
     corner_recv,
-    onward_send,
-    onward_recv,
 ):
     gx = lax.axis_index("gx")
     gy = lax.axis_index("gy")
@@ -168,7 +171,8 @@
     counts_copy = pltpu.make_async_copy(counts_hbm, counts, counts_sem)
     counts_copy.start()
     barrier = pltpu.get_barrier_semaphore()
-    partners = [(gx, peers[d]) for d in range(1, ny)] + [(left, gy), (right, gy)]
+    partners = [(gx, peers[d]) for d in range(1, ny)]
+    partners += [(x, y) for x in (left, right) for y in (gy, up, down)]
     for partner in partners:
         pl.semaphore_signal(barrier, inc=1, device_id=partner, device_id_type=MESH)
 
@@ -196,8 +200,8 @@
     load = class_load(counts[...], 128)
     load = jnp.where(row % 8 == (lane % 64) // 8, load, 0.0)
     slot, cell = iota((64, 256), 0), iota((64, 256), 1)
-    wanted = ((slot % 8) // 2) * 16 + 2 * (slot // 8) + slot % 2
-    pick = jnp.where((slot % 8 < 4) & (cell // 8 == wanted), 1.0, 0.0)
+    wanted = ((slot % 8) // 4) * 16 + (2 * (slot // 8) + 15 + slot % 4) % 16
+    pick = jnp.where(cell // 8 == wanted, 1.0, 0.0)
     load = jnp.dot(pick, load, precision=HIGH, preferred_element_type=F32)
     rate_out[...] = (1.0 / relax_time(load)).reshape(8, 8, 128)
     rate_in[pl.ds(gy, 1)] = rate_out[pl.ds(gy, 1)]
@@ -220,48 +224,62 @@
     heat_acc[...] = jnp.zeros_like(heat_acc)
     sums_out[...] = jnp.zeros_like(sums_out)
 
-    def prepare(kind, side, tile):
+    def prepare_y(tile, carry):
         lanes = pl.ds(pl.multiple_of(tile * 128, 128), 128)
-        leave = (LEAVE_X if kind == 0 else LEAVE_Y)[side]
-        plane = 15 if side == 0 else 0
-        for part in range(2):
-            rows = slice(8 * part, 8 * part + 8)
-            if kind == 0:
-                f = [pops[index, plane, rows, lanes] for index in range(19)]
-                fluid = solid[plane, rows, lanes] == 0
-            else:
+        for side in range(2):
+            for part in range(2):
+                rows = slice(8 * part, 8 * part + 8)
                 f = [row_pops[side, index, rows, lanes] for index in range(19)]
                 fluid = row_solid[side, rows, lanes] == 0
-            _, _, rho, (jx, jy, jz) = moments_of(f)
-            inverse = 1.0 / rho
-            terms = equilibrium(rho * 0.125, jx * inverse, jy * inverse, jz * inverse)
-            for place, index in enumerate(leave):
-                start_out[kind, side, place, rows, lanes] = jnp.where(
-                    fluid, f[index], f[opposite[index]]
-                )
-                gain_out[kind, side, place, rows, lanes] = jnp.where(
-                    fluid, equilibrium_of(index, terms) - f[index], 0.0
-                )
+                _, _, rho, flow = moments_of(f)
+                inverse = 1.0 / rho
+                for place, index in enumerate(LEAVE_Y[side]):
+                    y_out[side, place, rows, lanes] = jnp.where(fluid, f[index], f[opposite[index]])
+                y_out[side, 5, rows, lanes] = jnp.where(fluid, rho, 0.0)
+                for axis in range(3):
+                    y_out[side, 6 + axis, rows, lanes] = flow[axis] * inverse
+        return carry
+
+    def y_copy(side):
+        return pltpu.make_async_remote_copy(
+            src_ref=y_out.at[side],
+            dst_ref=y_in.at[side],
+            send_sem=y_send.at[side],
+            recv_sem=y_recv.at[side],
+            device_id=(gx, up if side == 0 else down),
+            device_id_type=MESH,
+        )
 
     for side in range(2):
         for copy in row_copies(side):
             copy.wait()
-
-    def prepare_y(tile, carry):
+    lax.fori_loop(0, 4, prepare_y, 0)
+    for side in range(2):
+        y_copy(side).start()
+
+    def prepare_x(tile, carry):
+        lanes = pl.ds(pl.multiple_of(tile * 128, 128), 128)
         for side in range(2):
-            prepare(1, side, tile)
+            plane = 15 if side == 0 else 0
+            for part in range(2):
+                rows = slice(8 * part, 8 * part + 8)
+                f = [pops[index, plane, rows, lanes] for index in range(19)]
+                fluid = solid[plane, rows, lanes] == 0
+                _, _, rho, (jx, jy, jz) = moments_of(f)
+                inverse = 1.0 / rho
+                terms = equilibrium(rho * 0.125, jx * inverse, jy * inverse, jz * inverse)
+                for place, index in enumerate(LEAVE_X[side]):
+                    start_out[side, place, rows, lanes] = jnp.where(
+                        fluid, f[index], f[opposite[index]]
+                    )
+                    gain_out[side, place, rows, lanes] = jnp.where(
+                        fluid, equilibrium_of(index, terms) - f[index], 0.0
+                    )
         return carry
-
-    lax.fori_loop(0, 4, prepare_y, 0)
 
     solid_copy.wait()
     for chunk in (0, 7):
         chunk_copy(chunk).wait()
-
-    def prepare_x(tile, carry):
-        for side in range(2):
-            prepare(0, side, tile)
-        return carry
 
     lax.fori_loop(0, 4, prepare_x, 0)
 
@@ -318,81 +336,55 @@
     lane = iota((8, 128), 1)
     for tile in range(4):
         owned = jnp.where(lane < 64, rate_in[2 * tile], rate_in[2 * tile + 1])
-        for block in range(4):
+        for block in range(8):
             rates[block, tile] = jnp.broadcast_to(owned[block : block + 1], (8, 128))
 
-    def edge_copy(kind, side, place):
-        index = (LEAVE_X if kind == 0 else LEAVE_Y)[side][place]
-        source = edge_out.at[kind, side, place]
-        if kind == 0:
-            target = moved.at[index, 1 if side == 0 else 16]
-            device = (right if side == 0 else left, gy)
-        else:
-            first = 1 + velocities[index][0]
-            target = moved.at[index, first : first + 16, 0 if side == 0 else 15]
-            device = (gx, up if side == 0 else down)
+    def edge_copy(side, place):
         return pltpu.make_async_remote_copy(
-            src_ref=source,
-            dst_ref=target,
-            send_sem=edge_send.at[kind, side, place],
-            recv_sem=edge_recv.at[kind, side, place],
-            device_id=device,
+            src_ref=edge_out.at[side, place],
+            dst_ref=moved.at[LEAVE_X[side][place], 1 if side == 0 else 16],
+            send_sem=edge_send.at[side, place],
+            recv_sem=edge_recv.at[side, place],
+            device_id=(right if side == 0 else left, gy),
             device_id_type=MESH,
         )
 
     def corner_copy(slot):
-        index, side, step = CORNERS[slot]
+        index, step_x, step_y = CORNERS[slot]
+        side = 0 if step_x > 0 else 1
         return pltpu.make_async_remote_copy(
-            src_ref=edge_out.at[1, side, LEAVE_Y[side].index(index), 15 if step > 0 else 0],
+            src_ref=edge_out.at[side, LEAVE_X[side].index(index), 0 if step_y > 0 else 15],
             dst_ref=corner_in.at[slot, 0],
             send_sem=corner_send.at[slot],
             recv_sem=corner_recv.at[slot],
-            device_id=(right if step > 0 else left, gy),
+            device_id=(right if step_x > 0 else left, up if step_y > 0 else down),
             device_id_type=MESH,
         )
 
-    def onward_copy(slot):
-        _, side, _ = CORNERS[slot]
-        return pltpu.make_async_remote_copy(
-            src_ref=corner_in.at[slot, 0],
-            dst_ref=corner_own.at[slot, 0],
-            send_sem=onward_send.at[slot],
-            recv_sem=onward_recv.at[slot],
-            device_id=(gx, up if side == 0 else down),
-            device_id_type=MESH,
-        )
-
-    def leave(kind, side, place):
-        index = (LEAVE_X if kind == 0 else LEAVE_Y)[side][place]
-        c = velocities[index]
+    def leave(side, place):
+        c = velocities[LEAVE_X[side][place]]
         values = []
         for part in range(2):
             rows = slice(8 * part, 8 * part + 8)
-            far = 1 - side
-            blocks = far * 2 + part if kind == 0 else part * 2 + far
+            block = (1 - side) * 4 + 1 + part
             tiles = [
-                start_out[kind, side, place, rows, TILES[t]]
-                + rates[blocks, t] * gain_out[kind, side, place, rows, TILES[t]]
+                start_out[side, place, rows, TILES[t]]
+                + rates[block, t] * gain_out[side, place, rows, TILES[t]]
                 for t in range(4)
             ]
             values.append(along_lanes(tiles, c[2]))
         for t in range(4):
-            low, high = along_rows(values[0][t], values[1][t], c[1] if kind == 0 else 0)
-            edge_out[kind, side, place, 0:8, TILES[t]] = low
-            edge_out[kind, side, place, 8:16, TILES[t]] = high
-
-    for slot, (index, side, _) in enumerate(CORNERS):
-        leave(1, side, LEAVE_Y[side].index(index))
-        corner_copy(slot).start()
-    for place in range(5):
-        for side in range(2):
-            leave(0, side, place)
-            edge_copy(0, side, place).start()
+            low, high = along_rows(values[0][t], values[1][t], c[1])
+            edge_out[side, place, 0:8, TILES[t]] = low
+            edge_out[side, place, 8:16, TILES[t]] = high
+
     for place in (1, 2, 0, 3, 4):
         for side in range(2):
-            if (LEAVE_Y[side][place], side) not in [corner[:2] for corner in CORNERS]:
-                leave(1, side, place)
-            edge_copy(1, side, place).start()
+            leave(side, place)
+            for slot, corner in enumerate(CORNERS):
+                if corner[0] == LEAVE_X[side][place]:
+                    corner_copy(slot).start()
+            edge_copy(side, place).start()
 
     for tile in range(4):
         sums_out[tile, 0:4, :] = jnp.sum(heat_acc[:, tile], axis=1)
@@ -415,14 +407,8 @@
         c = velocities[index]
         place, lanes = plane + 1 + c[0], TILES[tile]
         low, high = along_rows(low, high, c[1])
-        if c[1] > 0:
-            moved[index, place, 1:8, lanes] = low[1:8]
-        else:
-            moved[index, place, 0:8, lanes] = low
-        if c[1] < 0:
-            moved[index, place, 8:15, lanes] = high[0:7]
-        else:
-            moved[index, place, 8:16, lanes] = high
+        moved[index, place, 0:8, lanes] = low
+        moved[index, place, 8:16, lanes] = high
 
     def collide(plane):
         half = plane // 8
@@ -432,7 +418,7 @@
             for part in range(2):
                 rows = slice(8 * part, 8 * part + 8)
                 rho, ux, uy, uz = [moments[slot, plane, rows, lanes] for slot in range(4)]
-                rate = rates[half * 2 + part, tile]
+                rate = rates[half * 4 + 1 + part, tile]
                 terms = equilibrium((rate * 0.125) * rho, ux, uy, uz)
                 fluid = solid[plane, rows, lanes] == 0
                 kept = 1.0 - rate
@@ -467,45 +453,58 @@
         collide(plane)
         return carry
 
-    def some_planes(half, carry):
-        lax.fori_loop(1 + 8 * half, 9 + 7 * half, planes, 0)
-
-        @pl.when(half == 0)
-        def _():
-            for slot in range(4):
-                corner_copy(slot).wait_recv()
-                onward_copy(slot).start()
-
-        return carry
-
-    lax.fori_loop(0, 2, some_planes, 0)
+    lax.fori_loop(1, 16, planes, 0)
     run_z(15)
 
-    for kind in range(2):
-        for side in range(2):
-            for place in range(5):
-                edge_copy(kind, side, place).wait_recv()
-    for slot, (index, side, step) in enumerate(CORNERS):
-        onward_copy(slot).wait_recv()
-        row = 0 if side == 0 else 15
-        moved[index, 1 if step > 0 else 16, row : row + 1, :] = corner_own[slot, 0:1, :]
+    def collide_y(side):
+        y_copy(side).wait_recv()
+        found = [[[None] * 4 for _ in range(2)] for _ in range(5)]
+        for tile in range(4):
+            for part in range(2):
+                rows = slice(8 * part, 8 * part + 8)
+                rate = rates[part * 4 + 3 * side, tile]
+                rho, ux, uy, uz = [y_in[side, 5 + n, rows, TILES[tile]] for n in range(4)]
+                terms = equilibrium((rate * 0.125) * rho, ux, uy, uz)
+                kept = jnp.where(rho == 0.0, 1.0, 1.0 - rate)
+                for place, index in enumerate(LEAVE_Y[side]):
+                    found[place][part][tile] = kept * y_in[
+                        side, place, rows, TILES[tile]
+                    ] + equilibrium_of(index, terms)
+        for place, index in enumerate(LEAVE_Y[side]):
+            c = velocities[index]
+            low, high = [along_lanes(found[place][part], c[2]) for part in range(2)]
+            for t in range(4):
+                first, second = along_rows(low[t], high[t], c[0])
+                y_rows[side, place, 0:8, TILES[t]] = first
+                y_rows[side, place, 8:16, TILES[t]] = second
+
+    for side in range(2):
+        collide_y(side)
+    for slot, (index, step_x, step_y) in enumerate(CORNERS):
+        corner_copy(slot).wait_recv()
+        side, row = (0 if step_y > 0 else 1), (0 if step_x > 0 else 15)
+        y_rows[side, LEAVE_Y[side].index(index), row : row + 1, :] = corner_in[slot, 0:1, :]
+
+    for side in range(2):
+        for place in range(5):
+            edge_copy(side, place).wait_recv()
     for d in range(1, ny):
         sums_copy(d).wait_recv()
 
     for d in range(1, ny):
         rate_copy(d).wait_send()
         sums_copy(d).wait_send()
-    for kind in range(2):
-        for side in range(2):
-            for place in range(5):
-                edge_copy(kind, side, place).wait_send()
+    for side in range(2):
+        y_copy(side).wait_send()
+        for place in range(5):
+            edge_copy(side, place).wait_send()
     for slot in range(4):
         corner_copy(slot).wait_send()
-        onward_copy(slot).wait_send()
 
 
 def finish_kernel(
     moved,
+    y_rows,
     sums_in,
     counts_hbm,
     breakage_hbm,
@@ -518,11 +517,19 @@
     result,
     small_sem,
     read_sem,
+    row_sem,
     next_sem,
 ):
     copies = [
         pltpu.make_async_copy(moved.at[index, 1:17], read_hbm.at[index], read_sem.at[index])
-        for index in range(19)
+        for index in LEAVE_Y[0] + LEAVE_Y[1] + FLAT
+    ]
+    rows = [
+        pltpu.make_async_copy(
+            y_rows.at[side, place], read_hbm.at[index, :, 15 * side], row_sem.at[side, place]
+        )
+        for side in range(2)
+        for place, index in enumerate(LEAVE_Y[side])
     ]
     loads = [
         pltpu.make_async_copy(counts_hbm, counts, small_sem.at[0]),
@@ -561,11 +568,15 @@
             preferred_element_type=F32,
         )
         current = current + 0.25 * (born - lost)
+    for copy in copies[:10]:
+        copy.wait()
+    for copy in rows:
+        copy.start()
     result[...] = current
     last = pltpu.make_async_copy(result, next_hbm, next_sem)
     last.start()
     last.wait()
-    for copy in copies:
+    for copy in copies[10:] + rows:
         copy.wait()
 
 
@@ -574,14 +585,15 @@
     any_space = pl.BlockSpec(memory_space=pl.ANY)
     vmem = pl.BlockSpec(memory_space=pltpu.VMEM)
     dma = pltpu.SemaphoreType.DMA
-    moved, sums = pl.pallas_call(
+    moved, rows, sums = pl.pallas_call(
         functools.partial(step_kernel, nx, ny),
         out_shape=(
             pltpu.VMEM((19, 18, 16, 512), F32),
+            pltpu.VMEM((2, 5, 16, 512), F32),
             pltpu.VMEM((8, 8, 128), F32),
         ),
         in_specs=[any_space] * 3,
-        out_specs=(vmem, vmem),
+        out_specs=(vmem, vmem, vmem),
         scratch_shapes=[
             pltpu.VMEM((19, 16, 16, 512), F32),
             pltpu.VMEM((16, 16, 512), jnp.int32),
@@ -591,14 +603,15 @@
             pltpu.VMEM((4, 8, 128), F32),
             pltpu.VMEM((8, 8, 128), F32),
             pltpu.VMEM((8, 8, 128), F32),
-            pltpu.VMEM((4, 4, 8, 128), F32),
+            pltpu.VMEM((8, 4, 8, 128), F32),
             pltpu.VMEM((10, 16, 512), F32),
             pltpu.VMEM((2, 19, 16, 512), F32),
             pltpu.VMEM((2, 16, 512), jnp.int32),
-            pltpu.VMEM((2, 2, 5, 16, 512), F32),
-            pltpu.VMEM((2, 2, 5, 16, 512), F32),
-            pltpu.VMEM((2, 2, 5, 16, 512), F32),
-            pltpu.VMEM((4, 8, 512), F32),
+            pltpu.VMEM((2, 5, 16, 512), F32),
+            pltpu.VMEM((2, 5, 16, 512), F32),
+            pltpu.VMEM((2, 5, 16, 512), F32),
+            pltpu.VMEM((2, 9, 16, 512), F32),
+            pltpu.VMEM((2, 9, 16, 512), F32),
             pltpu.VMEM((4, 8, 512), F32),
             dma((8,)),
             dma,
@@ -608,10 +621,10 @@
             dma((8,)),
             dma((8,)),
             dma((8,)),
-            dma((2, 2, 5)),
-            dma((2, 2, 5)),
-            dma((4,)),
-            dma((4,)),
+            dma((2, 5)),
+            dma((2, 5)),
+            dma((2,)),
+            dma((2,)),
             dma((4,)),
             dma((4,)),
         ],
@@ -626,7 +639,7 @@
             jax.ShapeDtypeStruct(populations.shape, F32),
             jax.ShapeDtypeStruct(cells.shape, F32),
         ),
-        in_specs=[vmem] * 2 + [any_space] * 3,
+        in_specs=[vmem] * 3 + [any_space] * 3,
         out_specs=(any_space, any_space),
         scratch_shapes=[
             pltpu.VMEM((256, 64), F32),
@@ -635,11 +648,12 @@
             pltpu.VMEM((256, 64), F32),
             dma((3,)),
             dma((19,)),
+            dma((2, 5)),
             dma,
         ],
         compiler_params=pltpu.CompilerParams(vmem_limit_bytes=24 * 1024 * 1024),
         name="finish",
-    )(moved, sums, cells, breakage, selection)
+    )(moved, rows, sums, cells, breakage, selection)
     return (read, after.reshape(2, 16, 8, 64).transpose(3, 0, 1, 2))
 
 

time: 26.6 us -> 25.7 us (0.966)
  Pallas kernels: 25.7 us -> 24.9 us
    pallas_call x1, Pallas kernels: 21.7 us -> 20.7 us  [per_device(): pl.pallas_call(functools.partial(step_kernel, nx, ny), out_shape=(pltpu.V...]
where the time goes in v3:
time: 25.7 us; the launch traced here: 25.5 us
  Pallas kernels  24.9 us (97%)
  between operations  0.69 us (3%)
    pallas_call x1, Pallas kernels, per_device(): pl.pallas_call(functools.partial(step_kernel, nx, ny), out_shape=(pltpu.V...  20.7 us
    pallas_call x1, Pallas kernels, per_device(): pl.pallas_call(finish_kernel, out_shape=(jax.ShapeDtypeStruct(populations...  4.19 us

profile of v3, /device:TPU:0, one launch (start us, length us, event | category | flops | bytes accessed | tf_op | source)
XLA Modules:
  0.0 25.5 jit_solution(15372383058243681178)
XLA Ops:
  0.6 0.0 copy-start.2
  0.6 0.0 copy-start.1
  0.7 0.0 copy-start
  0.7 20.7 %collide.1 = (f32[19,18,16,512]{3,2,1,0:T(8,128)S(1)}, f32[2,5,16,512]{3,2,1,0:T(8,128)S(1)}, f32[8,8,128]{2,1,0:T(8,128)S(1)}) custom-call(f32[19,16,16,512]{3,2,1,0:T(8,128)} %pop_hbm.1, s32[16,16,512]{2,1,0:T(8,128)} %solid_hbm.1, f32[256,64]{1,0:T(8,128)} %bitcast.6), custom_call_target="tpu_custom_call" | custom-call | tf_op jit(solution)/shard_map/collide/pallas_call | solution.py:588
  21.3 0.0 copy-done.2
  21.3 0.0 copy-done.1
  21.4 0.0 copy-done
  21.4 4.2 %finish.1 = (f32[19,16,16,512]{3,2,1,0:T(8,128)}, f32[256,64]{1,0:T(8,128)}) custom-call(f32[19,18,16,512]{3,2,1,0:T(8,128)S(1)} %get-tuple-element.7.moved, f32[2,5,16,512]{3,2,1,0:T(8,128)S(1)} %get-tuple-element.8.y_rows, f32[8,8,128]{2,1,0:T(8,128)S(1)} %get-tuple-element.9.sums_in, f32[256,64]{1,0:T(8,128)S(1)} %bitcast.7, f32[64,64]{1,0:T(8,128)S(1)} %copy-done.1, ...), custom_call_target="tpu_custom_call" | custom-call | tf_op jit(solution)/shard_map/finish/pallas_call | solution.py:636
Async XLA Ops:
  0.6 20.7 %copy-start.2 = (f32[64]{0:T(128)S(1)}, f32[64]{0:T(128)}, u32[]{:S(2)}) copy-start(f32[64]{0:T(128)} %selection_hbm.1) | copy-start | bytes 772
  0.6 20.7 %copy-start.1 = (f32[64,64]{1,0:T(8,128)S(1)}, f32[64,64]{1,0:T(8,128)}, u32[]{:S(2)}) copy-start(f32[64,64]{1,0:T(8,128)} %breakage_hbm.1) | copy-start | bytes 49156
  0.7 20.7 %copy-start = (f32[64,2,16,8]{0,3,2,1:T(8,128)S(1)}, f32[64,2,16,8]{0,3,2,1:T(8,128)}, u32[]{:S(2)}) copy-start(f32[64,2,16,8]{0,3,2,1:T(8,128)} %param.7) | copy-start | bytes 196612

commit v4 on v3

--- a/solution.py
+++ b/solution.py
@@ -38,7 +38,7 @@
 LEAVE_X = ((1, 7, 9, 11, 13), (2, 8, 10, 12, 14))
 LEAVE_Y = ((3, 7, 10, 15, 17), (4, 8, 9, 16, 18))
 LEAVE_Z = (5, 6, 11, 12, 13, 14, 15, 16, 17, 18)
-CORNERS = ((7, 1, 1), (10, -1, 1), (9, 1, -1), (8, -1, -1))
+CORNERS = {7: (0, 0), 10: (0, 1), 9: (1, 0), 8: (1, 1)}
 FLAT = tuple(i for i in range(19) if velocities[i][1] == 0)
 TILES = tuple(slice(128 * t, 128 * t + 128) for t in range(4))
 
@@ -146,7 +146,7 @@
     edge_out,
     y_out,
     y_in,
-    corner_in,
+    ends_in,
     pop_sem,
     solid_sem,
     counts_sem,
@@ -159,8 +159,8 @@
     edge_recv,
     y_send,
     y_recv,
-    corner_send,
-    corner_recv,
+    ends_send,
+    ends_recv,
 ):
     gx = lax.axis_index("gx")
     gy = lax.axis_index("gy")
@@ -172,7 +172,7 @@
     counts_copy.start()
     barrier = pltpu.get_barrier_semaphore()
     partners = [(gx, peers[d]) for d in range(1, ny)]
-    partners += [(x, y) for x in (left, right) for y in (gy, up, down)]
+    partners += [(left, gy), (right, gy)]
     for partner in partners:
         pl.semaphore_signal(barrier, inc=1, device_id=partner, device_id_type=MESH)
 
@@ -205,21 +205,6 @@
     load = jnp.dot(pick, load, precision=HIGH, preferred_element_type=F32)
     rate_out[...] = (1.0 / relax_time(load)).reshape(8, 8, 128)
     rate_in[pl.ds(gy, 1)] = rate_out[pl.ds(gy, 1)]
-
-    pl.semaphore_wait(barrier, len(partners))
-
-    def rate_copy(d):
-        return pltpu.make_async_remote_copy(
-            src_ref=rate_out.at[peers[d]],
-            dst_ref=rate_in.at[gy],
-            send_sem=rate_send.at[d],
-            recv_sem=rate_recv.at[d],
-            device_id=(gx, peers[d]),
-            device_id_type=MESH,
-        )
-
-    for d in range(1, ny):
-        rate_copy(d).start()
 
     heat_acc[...] = jnp.zeros_like(heat_acc)
     sums_out[...] = jnp.zeros_like(sums_out)
@@ -254,6 +239,35 @@
         for copy in row_copies(side):
             copy.wait()
     lax.fori_loop(0, 4, prepare_y, 0)
+
+    pl.semaphore_wait(barrier, len(partners))
+
+    def rate_copy(d):
+        return pltpu.make_async_remote_copy(
+            src_ref=rate_out.at[peers[d]],
+            dst_ref=rate_in.at[gy],
+            send_sem=rate_send.at[d],
+            recv_sem=rate_recv.at[d],
+            device_id=(gx, peers[d]),
+            device_id_type=MESH,
+        )
+
+    for d in range(1, ny):
+        rate_copy(d).start()
+
+    def ends_copy(side, end):
+        return pltpu.make_async_remote_copy(
+            src_ref=y_out.at[side, :, 15 - 15 * end],
+            dst_ref=ends_in.at[side, end],
+            send_sem=ends_send.at[side, end],
+            recv_sem=ends_recv.at[side, end],
+            device_id=(gx, up if side == 0 else down),
+            device_id_type=MESH,
+        )
+
+    for side in range(2):
+        for end in range(2):
+            ends_copy(side, end).start()
     for side in range(2):
         y_copy(side).start()
 
@@ -349,18 +363,6 @@
             device_id_type=MESH,
         )
 
-    def corner_copy(slot):
-        index, step_x, step_y = CORNERS[slot]
-        side = 0 if step_x > 0 else 1
-        return pltpu.make_async_remote_copy(
-            src_ref=edge_out.at[side, LEAVE_X[side].index(index), 0 if step_y > 0 else 15],
-            dst_ref=corner_in.at[slot, 0],
-            send_sem=corner_send.at[slot],
-            recv_sem=corner_recv.at[slot],
-            device_id=(right if step_x > 0 else left, up if step_y > 0 else down),
-            device_id_type=MESH,
-        )
-
     def leave(side, place):
         c = velocities[LEAVE_X[side][place]]
         values = []
@@ -378,12 +380,26 @@
             edge_out[side, place, 0:8, TILES[t]] = low
             edge_out[side, place, 8:16, TILES[t]] = high
 
-    for place in (1, 2, 0, 3, 4):
+    def leave_corner(index):
+        from_y, side = CORNERS[index]
+        ends_copy(from_y, side).wait_recv()
+        row = 15 * from_y
+        for t in range(4):
+            cells = ends_in[from_y, side, :, TILES[t]]
+            rate = rates[4 * (1 - side) + 3 * from_y, t, 0:1]
+            rho, ux, uy, uz = [cells[n : n + 1] for n in range(5, 9)]
+            terms = equilibrium((rate * 0.125) * rho, ux, uy, uz)
+            kept = jnp.where(rho == 0.0, 1.0, 1.0 - rate)
+            place = LEAVE_Y[from_y].index(index)
+            edge_out[side, LEAVE_X[side].index(index), row : row + 1, TILES[t]] = kept * cells[
+                place : place + 1
+            ] + equilibrium_of(index, terms)
+
+    for place in (0, 3, 4, 1, 2):
         for side in range(2):
             leave(side, place)
-            for slot, corner in enumerate(CORNERS):
-                if corner[0] == LEAVE_X[side][place]:
-                    corner_copy(slot).start()
+            if LEAVE_X[side][place] in CORNERS:
+                leave_corner(LEAVE_X[side][place])
             edge_copy(side, place).start()
 
     for tile in range(4):
@@ -480,14 +496,14 @@
 
     for side in range(2):
         collide_y(side)
-    for slot, (index, step_x, step_y) in enumerate(CORNERS):
-        corner_copy(slot).wait_recv()
-        side, row = (0 if step_y > 0 else 1), (0 if step_x > 0 else 15)
-        y_rows[side, LEAVE_Y[side].index(index), row : row + 1, :] = corner_in[slot, 0:1, :]
-
     for side in range(2):
         for place in range(5):
             edge_copy(side, place).wait_recv()
+    for index, (from_y, side) in CORNERS.items():
+        row, end, plane = 15 * from_y, 15 * side, 1 + 15 * side
+        y_rows[from_y, LEAVE_Y[from_y].index(index), end : end + 1, :] = moved[
+            index, plane, row : row + 1, :
+        ]
     for d in range(1, ny):
         sums_copy(d).wait_recv()
 
@@ -498,8 +514,8 @@
         y_copy(side).wait_send()
         for place in range(5):
             edge_copy(side, place).wait_send()
-    for slot in range(4):
-        corner_copy(slot).wait_send()
+        for end in range(2):
+            ends_copy(side, end).wait_send()
 
 
 def finish_kernel(
@@ -612,7 +628,7 @@
             pltpu.VMEM((2, 5, 16, 512), F32),
             pltpu.VMEM((2, 9, 16, 512), F32),
             pltpu.VMEM((2, 9, 16, 512), F32),
-            pltpu.VMEM((4, 8, 512), F32),
+            pltpu.VMEM((2, 2, 9, 512), F32),
             dma((8,)),
             dma,
             dma,
@@ -625,8 +641,8 @@
             dma((2, 5)),
             dma((2,)),
             dma((2,)),
-            dma((4,)),
-            dma((4,)),
+            dma((2, 2)),
+            dma((2, 2)),
         ],
         compiler_params=pltpu.CompilerParams(
             collective_id=0, has_side_effects=True, vmem_limit_bytes=40 * 1024 * 1024

time: 25.7 us -> 26.4 us (1.027)
  Pallas kernels: 24.9 us -> 25.5 us
    pallas_call x1, Pallas kernels: 20.7 us -> 21.3 us  [per_device(): pl.pallas_call(functools.partial(step_kernel, nx, ny), out_shape=(pltpu.V...]
where the time goes in v4:
time: 26.4 us; the launch traced here: 26.2 us
  Pallas kernels  25.5 us (97%)
  between operations  0.69 us (3%)
    pallas_call x1, Pallas kernels, per_device(): pl.pallas_call(functools.partial(step_kernel, nx, ny), out_shape=(pltpu.V...  21.3 us
    pallas_call x1, Pallas kernels, per_device(): pl.pallas_call(finish_kernel, out_shape=(jax.ShapeDtypeStruct(populations...  4.19 us

profile of v4, /device:TPU:0, one launch (start us, length us, event | category | flops | bytes accessed | tf_op | source)
XLA Modules:
  0.0 26.2 jit_solution(2684175770971337144)
XLA Ops:
  0.6 0.0 copy-start.2
  0.6 0.0 copy-start.1
  0.7 0.0 copy-start
  0.7 21.3 %collide.1 = (f32[19,18,16,512]{3,2,1,0:T(8,128)S(1)}, f32[2,5,16,512]{3,2,1,0:T(8,128)S(1)}, f32[8,8,128]{2,1,0:T(8,128)S(1)}) custom-call(f32[19,16,16,512]{3,2,1,0:T(8,128)} %pop_hbm.1, s32[16,16,512]{2,1,0:T(8,128)} %solid_hbm.1, f32[256,64]{1,0:T(8,128)} %bitcast.6), custom_call_target="tpu_custom_call" | custom-call | tf_op jit(solution)/shard_map/collide/pallas_call | solution.py:604
  22.0 0.0 copy-done.2
  22.0 0.0 copy-done.1
  22.0 0.0 copy-done
  22.0 4.2 %finish.1 = (f32[19,16,16,512]{3,2,1,0:T(8,128)}, f32[256,64]{1,0:T(8,128)}) custom-call(f32[19,18,16,512]{3,2,1,0:T(8,128)S(1)} %get-tuple-element.7.moved, f32[2,5,16,512]{3,2,1,0:T(8,128)S(1)} %get-tuple-element.8.y_rows, f32[8,8,128]{2,1,0:T(8,128)S(1)} %get-tuple-element.9.sums_in, f32[256,64]{1,0:T(8,128)S(1)} %bitcast.7, f32[64,64]{1,0:T(8,128)S(1)} %copy-done.1, ...), custom_call_target="tpu_custom_call" | custom-call | tf_op jit(solution)/shard_map/finish/pallas_call | solution.py:652
Async XLA Ops:
  0.6 21.3 %copy-start.2 = (f32[64]{0:T(128)S(1)}, f32[64]{0:T(128)}, u32[]{:S(2)}) copy-start(f32[64]{0:T(128)} %selection_hbm.1) | copy-start | bytes 772
  0.6 21.3 %copy-start.1 = (f32[64,64]{1,0:T(8,128)S(1)}, f32[64,64]{1,0:T(8,128)}, u32[]{:S(2)}) copy-start(f32[64,64]{1,0:T(8,128)} %breakage_hbm.1) | copy-start | bytes 49156
  0.7 21.3 %copy-start = (f32[64,2,16,8]{0,3,2,1:T(8,128)S(1)}, f32[64,2,16,8]{0,3,2,1:T(8,128)}, u32[]{:S(2)}) copy-start(f32[64,2,16,8]{0,3,2,1:T(8,128)} %param.7) | copy-start | bytes 196612

commit v5 on v1

v5 whole, which is shorter than its diff:
```python
import functools

import jax
import jax.numpy as jnp
from jax import lax
from jax.experimental import pallas as pl
from jax.experimental.pallas import tpu as pltpu
from jax.sharding import PartitionSpec as P

SUB = 4
MESH = pl.DeviceIdType.MESH
F32 = jnp.float32
HIGH = lax.Precision.HIGHEST

velocities = (
    (0, 0, 0),
    (1, 0, 0),
    (-1, 0, 0),
    (0, 1, 0),
    (0, -1, 0),
    (0, 0, 1),
    (0, 0, -1),
    (1, 1, 0),
    (-1, -1, 0),
    (1, -1, 0),
    (-1, 1, 0),
    (1, 0, 1),
    (-1, 0, -1),
    (1, 0, -1),
    (-1, 0, 1),
    (0, 1, 1),
    (0, -1, -1),
    (0, 1, -1),
    (0, -1, 1),
)
opposite = (0, 2, 1, 4, 3, 6, 5, 8, 7, 10, 9, 12, 11, 14, 13, 16, 15, 18, 17)

LEAVE_X = ((1, 7, 9, 11, 13), (2, 8, 10, 12, 14))
LEAVE_Y = ((3, 7, 10, 15, 17), (4, 8, 9, 16, 18))
LEAVE_Z = (5, 6, 11, 12, 13, 14, 15, 16, 17, 18)
CORNERS = {7: (0, 0), 10: (0, 1), 9: (1, 0), 8: (1, 1)}
TILES = tuple(slice(128 * t, 128 * t + 128) for t in range(4))


def iota(shape, axis):
    return lax.broadcasted_iota(jnp.int32, shape, axis)


def class_load(counts, lanes):
    volume = (iota((64, lanes), 0).astype(F32) + 1.0) / 64.0
    return jnp.dot(counts, volume, precision=HIGH, preferred_element_type=F32)


def relax_time(load):
    packed = 0.5 * load / (1.0 + load)
    thinned = 1.0 - packed / 0.64
    return 0.5 + 3.0 * (0.04 / (thinned * thinned))


def moments_of(f):
    even = {i: f[i] + f[i + 1] for i in range(1, 19, 2)}
    odd = {i: f[i] - f[i + 1] for i in range(1, 19, 2)}
    xy, xz, yz = even[7] + even[9], even[11] + even[13], even[15] + even[17]
    rho = f[0] + (even[1] + xy) + (even[3] + yz) + (even[5] + xz)
    jx = odd[1] + (odd[7] + odd[9]) + (odd[11] + odd[13])
    jy = odd[3] + (odd[7] - odd[9]) + (odd[15] + odd[17])
    jz = odd[5] + (odd[11] - odd[13]) + (odd[15] - odd[17])
    return even, (xy, xz, yz), rho, (jx, jy, jz)


def equilibrium(eighth, ux, uy, uz):
    tx, ty, tz = eighth * ux, eighth * uy, eighth * uz
    xx, yy, zz = tx * ux, ty * uy, tz * uz
    tx2, ty2 = tx + tx, ty + ty
    cross = (tx2 * uy, tx2 * uz, ty2 * uz)
    base = eighth * (8.0 / 36.0) - (xx + yy + zz) * (1.0 / 3.0)
    bx, by, bz = base + xx, base + yy, base + zz
    sums = (bx + yy, bx + zz, by + zz)
    return base, (bx, by, bz), sums, cross, (tx * (2.0 / 3.0), ty * (2.0 / 3.0), tz * (2.0 / 3.0))


def equilibrium_of(index, terms):
    base, axes, sums, cross, flow = terms
    c = velocities[index]
    nonzero = [a for a in range(3) if c[a] != 0]
    if not nonzero:
        return 12.0 * base
    if len(nonzero) == 1:
        (a,) = nonzero
        even = axes[a] + axes[a]
        odd = flow[a] + flow[a]
        return even + odd if c[a] > 0 else even - odd
    a, b = nonzero
    slot = {(0, 1): 0, (0, 2): 1, (1, 2): 2}[(a, b)]
    even = sums[slot] + cross[slot] if c[a] * c[b] > 0 else sums[slot] - cross[slot]
    odd = flow[a] + flow[b] if c[a] == c[b] else flow[a] - flow[b]
    return even + odd if c[a] > 0 else even - odd


def along_lanes(tiles, step):
    if step == 0:
        return tiles
    lane = iota((8, 128), 1)
    if step > 0:
        moved = [pltpu.roll(v, 1, 1) for v in tiles]
        return [jnp.where(lane == 0, moved[(t + 3) % 4], moved[t]) for t in range(4)]
    moved = [pltpu.roll(v, 127, 1) for v in tiles]
    return [jnp.where(lane == 127, moved[(t + 1) % 4], moved[t]) for t in range(4)]


def along_rows(low, high, step):
    if step == 0:
        return low, high
    row = iota((8, 128), 0)
    if step > 0:
        low, high = pltpu.roll(low, 1, 0), pltpu.roll(high, 1, 0)
        return jnp.where(row == 0, high, low), jnp.where(row == 0, low, high)
    low, high = pltpu.roll(low, 7, 0), pltpu.roll(high, 7, 0)
    return jnp.where(row == 7, high, low), jnp.where(row == 7, low, high)


def break_up(gy, counts, breakage, selection, sums_in, result):
    current = counts[...]
    tau = relax_time(class_load(current, 128))
    factor = (tau - 0.5) / (3.0 * tau * tau)
    row, slot = iota((256, 64), 0), iota((256, 64), 1)
    wanted = ((row // 8) % 16 // 2) * 8 + (row // 128) * 2 + (row // 8) % 2
    pick = jnp.where(slot == wanted, 1.0, 0.0)
    sums = jnp.dot(
        pick, sums_in[...].reshape(64, 128), precision=HIGH, preferred_element_type=F32
    )
    row, lane = iota((256, 128), 0), iota((256, 128), 1)
    sums = jnp.where(lane // 8 == row % 8 + 8 * lax.rem(gy, 2), sums, 0.0)
    sums = jnp.dot(sums, jnp.ones((128, 128), F32), precision=HIGH, preferred_element_type=F32)
    eps = sums * (4.5 / 512.0) * factor
    strength = jnp.sqrt(50.0 * eps + 1e-06)
    gain = strength / (1.0 + strength)
    rate = gain[:, :64] * selection[...][None, :]
    for step in range(SUB):
        lost = rate * current
        born = lax.dot_general(
            lost,
            breakage[...],
            (((1,), (1,)), ((), ())),
            precision=HIGH,
            preferred_element_type=F32,
        )
        current = current + 0.25 * (born - lost)
    result[...] = current


def step_kernel(
    nx,
    ny,
    pop_hbm,
    solid_hbm,
    counts_hbm,
    breakage_hbm,
    selection_hbm,
    moved,
    result,
    pops,
    solid,
    counts,
    breakage,
    selection,
    moments,
    heat_acc,
    sums_out,
    sums_in,
    rate_out,
    rate_in,
    rates,
    staged,
    row_pops,
    row_solid,
    start_out,
    gain_out,
    edge_out,
    y_out,
    ends_in,
    pop_sem,
    solid_sem,
    counts_sem,
    small_sem,
    row_sem,
    rate_send,
    rate_recv,
    sums_send,
    sums_recv,
    edge_send,
    edge_recv,
    ends_send,
    ends_recv,
):
    gx = lax.axis_index("gx")
    gy = lax.axis_index("gy")
    right, left = lax.rem(gx + 1, nx), lax.rem(gx + nx - 1, nx)
    up, down = lax.rem(gy + 1, ny), lax.rem(gy + ny - 1, ny)
    peers = [lax.rem(gy + d, ny) for d in range(ny)]

    counts_copy = pltpu.make_async_copy(counts_hbm, counts, counts_sem)
    counts_copy.start()
    barrier = pltpu.get_barrier_semaphore()
    partners = [(gx, peers[d]) for d in range(1, ny)]
    partners += [(left, gy), (right, gy)]
    for partner in partners:
        pl.semaphore_signal(barrier, inc=1, device_id=partner, device_id_type=MESH)

    def chunk_copy(chunk):
        rows = pl.ds(2 * chunk, 2)
        return pltpu.make_async_copy(pop_hbm.at[:, rows], pops.at[:, rows], pop_sem.at[chunk])

    def row_copies(side):
        y = 15 if side == 0 else 0
        return (
            pltpu.make_async_copy(solid_hbm.at[:, y], row_solid.at[side], row_sem.at[side, 0]),
            pltpu.make_async_copy(pop_hbm.at[:, :, y], row_pops.at[side], row_sem.at[side, 1]),
        )

    solid_copy = pltpu.make_async_copy(solid_hbm, solid, solid_sem)
    for side in range(2):
        for copy in row_copies(side):
            copy.start()
    solid_copy.start()
    for chunk in (0, 7, 1, 2):
        chunk_copy(chunk).start()
    small_copies = (
        pltpu.make_async_copy(breakage_hbm, breakage, small_sem.at[0]),
        pltpu.make_async_copy(selection_hbm, selection, small_sem.at[1]),
    )
    for copy in small_copies:
        copy.start()

    counts_copy.wait()
    row, lane = iota((256, 128), 0), iota((256, 128), 1)
    load = class_load(counts[...], 128)
    load = jnp.where(row % 8 == (lane % 64) // 8, load, 0.0)
    slot, cell = iota((64, 256), 0), iota((64, 256), 1)
    wanted = ((slot % 8) // 4) * 16 + (2 * (slot // 8) + 15 + slot % 4) % 16
    pick = jnp.where(cell // 8 == wanted, 1.0, 0.0)
    load = jnp.dot(pick, load, precision=HIGH, preferred_element_type=F32)
    rate_out[...] = (1.0 / relax_time(load)).reshape(8, 8, 128)
    rate_in[pl.ds(gy, 1)] = rate_out[pl.ds(gy, 1)]

    pl.semaphore_wait(barrier, len(partners))

    def rate_copy(d):
        return pltpu.make_async_remote_copy(
            src_ref=rate_out.at[peers[d]],
            dst_ref=rate_in.at[gy],
            send_sem=rate_send.at[d],
            recv_sem=rate_recv.at[d],
            device_id=(gx, peers[d]),
            device_id_type=MESH,
        )

    for d in range(1, ny):
        rate_copy(d).start()

    heat_acc[...] = jnp.zeros_like(heat_acc)
    sums_out[...] = jnp.zeros_like(sums_out)

    def prepare(kind, side, tile):
        lanes = pl.ds(pl.multiple_of(tile * 128, 128), 128)
        plane = 15 if side == 0 else 0
        for part in range(2):
            rows = slice(8 * part, 8 * part + 8)
            if kind == 0:
                f = [pops[index, plane, rows, lanes] for index in range(19)]
                fluid = solid[plane, rows, lanes] == 0
            else:
                f = [row_pops[side, index, rows, lanes] for index in range(19)]
                fluid = row_solid[side, rows, lanes] == 0
            _, _, rho, flow = moments_of(f)
            inverse = 1.0 / rho
            speed = [component * inverse for component in flow]
            terms = equilibrium(rho * 0.125, *speed)
            for place, index in enumerate((LEAVE_X if kind == 0 else LEAVE_Y)[side]):
                start = jnp.where(fluid, f[index], f[opposite[index]])
                start_out[kind, side, place, rows, lanes] = start
                gain_out[kind, side, place, rows, lanes] = jnp.where(
                    fluid, equilibrium_of(index, terms) - f[index], 0.0
                )
                if kind == 1:
                    y_out[side, place, rows, lanes] = start
            if kind == 1:
                y_out[side, 5, rows, lanes] = jnp.where(fluid, rho, 0.0)
                for axis in range(3):
                    y_out[side, 6 + axis, rows, lanes] = speed[axis]

    def prepare_y(tile, carry):
        for side in range(2):
            prepare(1, side, tile)
        return carry

    def prepare_x(tile, carry):
        for side in range(2):
            prepare(0, side, tile)
        return carry

    for side in range(2):
        for copy in row_copies(side):
            copy.wait()
    lax.fori_loop(0, 4, prepare_y, 0)

    def ends_copy(side, end):
        return pltpu.make_async_remote_copy(
            src_ref=y_out.at[side, :, 15 - 15 * end],
            dst_ref=ends_in.at[side, end],
            send_sem=ends_send.at[side, end],
            recv_sem=ends_recv.at[side, end],
            device_id=(gx, up if side == 0 else down),
            device_id_type=MESH,
        )

    for side in range(2):
        for end in range(2):
            ends_copy(side, end).start()

    solid_copy.wait()
    for chunk in (0, 7):
        chunk_copy(chunk).wait()

    lax.fori_loop(0, 4, prepare_x, 0)

    def first_pass(chunk):
        half = chunk // 4

        def one_tile(tile, carry):
            lanes = pl.ds(pl.multiple_of(tile * 128, 128), 128)
            heats = []
            for part in range(4):
                plane, rows = 2 * chunk + part // 2, slice(8 * (part % 2), 8 * (part % 2) + 8)
                f = [pops[index, plane, rows, lanes] for index in range(19)]
                even, (xy, xz, yz), rho, (jx, jy, jz) = moments_of(f)
                inverse = 1.0 / rho
                ux, uy, uz = jx * inverse, jy * inverse, jz * inverse
                third = rho * (1.0 / 3.0)
                pxx = even[1] + (xy + xz) - third - jx * ux
                pyy = even[3] + (xy + yz) - third - jy * uy
                pzz = even[5] + (xz + yz) - third - jz * uz
                pxy = even[7] - even[9] - jx * uy
                pxz = even[11] - even[13] - jx * uz
                pyz = even[15] - even[17] - jy * uz
                off = pxy * pxy + pxz * pxz + pyz * pyz
                square = pxx * pxx + pyy * pyy + pzz * pzz + (off + off)
                heat = square * (inverse * inverse)
                heats.append(jnp.where(solid[plane, rows, lanes] == 0, heat, 0.0))
                for slot, value in enumerate((rho, ux, uy, uz)):
                    moments[slot, plane, rows, lanes] = value
            heat_acc[half * 2, tile] += heats[0] + heats[2]
            heat_acc[half * 2 + 1, tile] += heats[1] + heats[3]
            return carry

        lax.fori_loop(0, 4, one_tile, 0)

    def outer_chunks(step, carry):
        first_pass(step * 7)
        return carry

    def inner_chunks(chunk, carry):
        chunk_copy(chunk).wait()

        @pl.when(chunk < 5)
        def _():
            chunk_copy(chunk + 2).start()

        first_pass(chunk)
        return carry

    lax.fori_loop(0, 2, outer_chunks, 0)
    lax.fori_loop(1, 7, inner_chunks, 0)

    for tile in range(4):
        sums_out[tile, 0:4, :] = jnp.sum(heat_acc[:, tile], axis=1)
    sums_in[pl.ds(gy, 1)] = sums_out[pl.ds(gy // 2, 1)]

    def sums_copy(d):
        return pltpu.make_async_remote_copy(
            src_ref=sums_out.at[peers[d] // 2],
            dst_ref=sums_in.at[gy],
            send_sem=sums_send.at[d],
            recv_sem=sums_recv.at[d],
            device_id=(gx, peers[d]),
            device_id_type=MESH,
        )

    for d in range(1, ny):
        sums_copy(d).start()

    for d in range(1, ny):
        rate_copy(d).wait_recv()
    lane = iota((8, 128), 1)
    for tile in range(4):
        owned = jnp.where(lane < 64, rate_in[2 * tile], rate_in[2 * tile + 1])
        for block in range(8):
            rates[block, tile] = jnp.broadcast_to(owned[block : block + 1], (8, 128))

    def edge_copy(kind, side, place):
        index = (LEAVE_X if kind == 0 else LEAVE_Y)[side][place]
        if kind == 0:
            target = moved.at[index, 1 if side == 0 else 16]
            device = (right if side == 0 else left, gy)
        else:
            first = 1 + velocities[index][0]
            target = moved.at[index, first : first + 16, 0 if side == 0 else 15]
            device = (gx, up if side == 0 else down)
        return pltpu.make_async_remote_copy(
            src_ref=edge_out.at[kind, side, place],
            dst_ref=target,
            send_sem=edge_send.at[kind, side, place],
            recv_sem=edge_recv.at[kind, side, place],
            device_id=device,
            device_id_type=MESH,
        )

    def leave(kind, side, place):
        c = velocities[(LEAVE_X if kind == 0 else LEAVE_Y)[side][place]]
        far = 1 - side
        values = []
        for part in range(2):
            rows = slice(8 * part, 8 * part + 8)
            block = far * 4 + 1 + part if kind == 0 else part * 4 + 1 + far
            tiles = [
                start_out[kind, side, place, rows, TILES[t]]
                + rates[block, t] * gain_out[kind, side, place, rows, TILES[t]]
                for t in range(4)
            ]
            values.append(along_lanes(tiles, c[2]))
        for t in range(4):
            low, high = along_rows(values[0][t], values[1][t], c[1] if kind == 0 else 0)
            edge_out[kind, side, place, 0:8, TILES[t]] = low
            edge_out[kind, side, place, 8:16, TILES[t]] = high

    def leave_corner(index):
        from_y, side = CORNERS[index]
        ends_copy(from_y, side).wait_recv()
        row = 15 * from_y
        for t in range(4):
            cells = ends_in[from_y, side, :, TILES[t]]
            rate = rates[4 * (1 - side) + 3 * from_y, t, 0:1]
            rho, ux, uy, uz = [cells[n : n + 1] for n in range(5, 9)]
            terms = equilibrium((rate * 0.125) * rho, ux, uy, uz)
            kept = jnp.where(rho == 0.0, 1.0, 1.0 - rate)
            place = LEAVE_Y[from_y].index(index)
            edge_out[0, side, LEAVE_X[side].index(index), row : row + 1, TILES[t]] = kept * cells[
                place : place + 1
            ] + equilibrium_of(index, terms)

    for place in (0, 3, 4, 1, 2):
        for side in range(2):
            leave(0, side, place)
            if LEAVE_X[side][place] in CORNERS:
                leave_corner(LEAVE_X[side][place])
            edge_copy(0, side, place).start()
    for place in range(5):
        for side in range(2):
            leave(1, side, place)
            edge_copy(1, side, place).start()

    def put(index, plane, tile, low, high):
        c = velocities[index]
        place, lanes = plane + 1 + c[0], TILES[tile]
        low, high = along_rows(low, high, c[1])
        if c[1] > 0:
            moved[index, place, 1:8, lanes] = low[1:8]
        else:
            moved[index, place, 0:8, lanes] = low
        if c[1] < 0:
            moved[index, place, 8:15, lanes] = high[0:7]
        else:
            moved[index, place, 8:16, lanes] = high

    def collide(plane):
        half = plane // 8
        for tile in range(4):
            lanes = TILES[tile]
            found = []
            for part in range(2):
                rows = slice(8 * part, 8 * part + 8)
                rho, ux, uy, uz = [moments[slot, plane, rows, lanes] for slot in range(4)]
                rate = rates[half * 4 + 1 + part, tile]
                terms = equilibrium((rate * 0.125) * rho, ux, uy, uz)
                fluid = solid[plane, rows, lanes] == 0
                kept = 1.0 - rate
                f = [pops[index, plane, rows, lanes] for index in range(19)]
                found.append(
                    [
                        jnp.where(
                            fluid, kept * f[index] + equilibrium_of(index, terms), f[opposite[index]]
                        )
                        for index in range(19)
                    ]
                )
            for index in range(19):
                low, high = found[0][index], found[1][index]
                if index in LEAVE_Z:
                    staged[LEAVE_Z.index(index), 0:8, lanes] = low
                    staged[LEAVE_Z.index(index), 8:16, lanes] = high
                else:
                    put(index, plane, tile, low, high)

    def run_z(plane):
        for place, index in enumerate(LEAVE_Z):
            low = along_lanes([staged[place, 0:8, TILES[t]] for t in range(4)], velocities[index][2])
            high = along_lanes([staged[place, 8:16, TILES[t]] for t in range(4)], velocities[index][2])
            for t in range(4):
                put(index, plane, t, low[t], high[t])

    collide(0)

    def planes(plane, carry):
        run_z(plane - 1)
        collide(plane)
        return carry

    lax.fori_loop(1, 16, planes, 0)
    run_z(15)

    for copy in small_copies:
        copy.wait()
    for d in range(1, ny):
        sums_copy(d).wait_recv()
    break_up(gy, counts, breakage, selection, sums_in, result)

    for kind in range(2):
        for side in range(2):
            for place in range(5):
                edge_copy(kind, side, place).wait_recv()

    for d in range(1, ny):
        rate_copy(d).wait_send()
        sums_copy(d).wait_send()
    for side in range(2):
        for place in range(5):
            for kind in range(2):
                edge_copy(kind, side, place).wait_send()
        for end in range(2):
            ends_copy(side, end).wait_send()


def finish_kernel(moved, result, read_hbm, next_hbm, read_sem, next_sem):
    copies = [
        pltpu.make_async_copy(moved.at[index, 1:17], read_hbm.at[index], read_sem.at[index])
        for index in range(19)
    ]
    copies.append(pltpu.make_async_copy(result, next_hbm, next_sem))
    for copy in copies:
        copy.start()
    for copy in copies:
        copy.wait()


def per_device(nx, ny, populations, solid, counts, breakage, selection):
    cells = counts.transpose(1, 2, 3, 0).reshape(256, 64)
    any_space = pl.BlockSpec(memory_space=pl.ANY)
    vmem = pl.BlockSpec(memory_space=pltpu.VMEM)
    dma = pltpu.SemaphoreType.DMA
    moved, result = pl.pallas_call(
        functools.partial(step_kernel, nx, ny),
        out_shape=(
            pltpu.VMEM((19, 18, 16, 512), F32),
            pltpu.VMEM((256, 64), F32),
        ),
        in_specs=[any_space] * 5,
        out_specs=(vmem, vmem),
        scratch_shapes=[
            pltpu.VMEM((19, 16, 16, 512), F32),
            pltpu.VMEM((16, 16, 512), jnp.int32),
            pltpu.VMEM((256, 64), F32),
            pltpu.VMEM((64, 64), F32),
            pltpu.VMEM((64,), F32),
            pltpu.VMEM((4, 16, 16, 512), F32),
            pltpu.VMEM((4, 4, 8, 128), F32),
            pltpu.VMEM((4, 8, 128), F32),
            pltpu.VMEM((8, 8, 128), F32),
            pltpu.VMEM((8, 8, 128), F32),
            pltpu.VMEM((8, 8, 128), F32),
            pltpu.VMEM((8, 4, 8, 128), F32),
            pltpu.VMEM((10, 16, 512), F32),
            pltpu.VMEM((2, 19, 16, 512), F32),
            pltpu.VMEM((2, 16, 512), jnp.int32),
            pltpu.VMEM((2, 2, 5, 16, 512), F32),
            pltpu.VMEM((2, 2, 5, 16, 512), F32),
            pltpu.VMEM((2, 2, 5, 16, 512), F32),
            pltpu.VMEM((2, 9, 16, 512), F32),
            pltpu.VMEM((2, 2, 9, 512), F32),
            dma((8,)),
            dma,
            dma,
            dma((2,)),
            dma((2, 2)),
            dma((8,)),
            dma((8,)),
            dma((8,)),
            dma((8,)),
            dma((2, 2, 5)),
            dma((2, 2, 5)),
            dma((2, 2)),
            dma((2, 2)),
        ],
        compiler_params=pltpu.CompilerParams(
            collective_id=0, has_side_effects=True, vmem_limit_bytes=40 * 1024 * 1024
        ),
        name="collide",
    )(
        *[
            pltpu.with_memory_space_constraint(x, pltpu.HBM)
            for x in (populations, solid, cells, breakage, selection)
        ]
    )
    read, after = pl.pallas_call(
        finish_kernel,
        out_shape=(
            jax.ShapeDtypeStruct(populations.shape, F32),
            jax.ShapeDtypeStruct(cells.shape, F32),
        ),
        in_specs=[vmem] * 2,
        out_specs=(any_space, any_space),
        scratch_shapes=[dma((19,)), dma],
        compiler_params=pltpu.CompilerParams(vmem_limit_bytes=24 * 1024 * 1024),
        name="finish",
    )(moved, result)
    return (read, after.reshape(2, 16, 8, 64).transpose(3, 0, 1, 2))


def solution(mesh):
    in_specs = (P(None, "gx", "gy", None), P("gx", "gy", None), P(None, "gx", None, "gy"), P(), P())
    out_specs = (P(None, "gx", "gy", None), P(None, "gx", None, "gy"))
    return jax.shard_map(
        functools.partial(per_device, mesh.shape["gx"], mesh.shape["gy"]),
        mesh=mesh,
        in_specs=in_specs,
        out_specs=out_specs,
        check_vma=False,
    )
```

time: 31.3 us -> 26.4 us (0.84)
  Pallas kernels: 30.5 us -> 25.6 us
    pallas_call x1, Pallas kernels: 26.3 us -> 21.6 us  [per_device(): pl.pallas_call(functools.partial(step_kernel, nx, ny), out_shape=(pltpu.V...]
where the time goes in v5:
time: 26.4 us; the launch traced here: 26.2 us
  Pallas kernels  25.6 us (97%)
  between operations  0.64 us (2%)
    pallas_call x1, Pallas kernels, per_device(): pl.pallas_call(functools.partial(step_kernel, nx, ny), out_shape=(pltpu.V...  21.6 us
    pallas_call x1, Pallas kernels, per_device(): pl.pallas_call(finish_kernel, out_shape=(jax.ShapeDtypeStruct(populations...  3.95 us

profile of v5, /device:TPU:0, one launch (start us, length us, event | category | flops | bytes accessed | tf_op | source)
XLA Modules:
  0.0 26.2 jit_solution(16602667773265131440)
XLA Ops:
  0.6 21.6 %collide.1 = (f32[19,18,16,512]{3,2,1,0:T(8,128)S(1)}, f32[256,64]{1,0:T(8,128)S(1)}) custom-call(f32[19,16,16,512]{3,2,1,0:T(8,128)} %pop_hbm.1, s32[16,16,512]{2,1,0:T(8,128)} %solid_hbm.1, f32[256,64]{1,0:T(8,128)} %bitcast.6, f32[64,64]{1,0:T(8,128)} %breakage_hbm.1, f32[64]{0:T(128)} %selection_hbm.1), custom_call_target="tpu_custom_call" | custom-call | tf_op jit(solution)/shard_map/collide/pallas_call | solution.py:560
  22.3 3.9 %finish.1 = (f32[19,16,16,512]{3,2,1,0:T(8,128)}, f32[256,64]{1,0:T(8,128)}) custom-call(f32[19,18,16,512]{3,2,1,0:T(8,128)S(1)} %get-tuple-element.6.moved, f32[256,64]{1,0:T(8,128)S(1)} %get-tuple-element.7.result), custom_call_target="tpu_custom_call" | custom-call | tf_op jit(solution)/shard_map/finish/pallas_call | solution.py:613

commit v6 on v5

--- a/solution.py
+++ b/solution.py
@@ -39,6 +39,7 @@
 LEAVE_Y = ((3, 7, 10, 15, 17), (4, 8, 9, 16, 18))
 LEAVE_Z = (5, 6, 11, 12, 13, 14, 15, 16, 17, 18)
 CORNERS = {7: (0, 0), 10: (0, 1), 9: (1, 0), 8: (1, 1)}
+EARLY = 5
 TILES = tuple(slice(128 * t, 128 * t + 128) for t in range(4))
 
 
@@ -183,6 +184,7 @@
     solid_sem,
     counts_sem,
     small_sem,
+    row_solid_sem,
     row_sem,
     rate_send,
     rate_recv,
@@ -207,24 +209,37 @@
     for partner in partners:
         pl.semaphore_signal(barrier, inc=1, device_id=partner, device_id_type=MESH)
 
-    def chunk_copy(chunk):
-        rows = pl.ds(2 * chunk, 2)
-        return pltpu.make_async_copy(pop_hbm.at[:, rows], pops.at[:, rows], pop_sem.at[chunk])
-
-    def row_copies(side):
+    def lanes_of(tile):
+        return pl.ds(pl.multiple_of(tile * 128, 128), 128)
+
+    def chunk_copy(chunk, tile):
+        rows, lanes = pl.ds(2 * chunk, 2), lanes_of(tile)
+        return pltpu.make_async_copy(
+            pop_hbm.at[:, rows, :, lanes], pops.at[:, rows, :, lanes], pop_sem.at[chunk, tile]
+        )
+
+    def row_solid_copy(side):
         y = 15 if side == 0 else 0
-        return (
-            pltpu.make_async_copy(solid_hbm.at[:, y], row_solid.at[side], row_sem.at[side, 0]),
-            pltpu.make_async_copy(pop_hbm.at[:, :, y], row_pops.at[side], row_sem.at[side, 1]),
+        return pltpu.make_async_copy(
+            solid_hbm.at[:, y], row_solid.at[side], row_solid_sem.at[side]
+        )
+
+    def row_copy(side, tile):
+        y, lanes = 15 if side == 0 else 0, lanes_of(tile)
+        return pltpu.make_async_copy(
+            pop_hbm.at[:, :, y, lanes], row_pops.at[side, :, :, lanes], row_sem.at[side, tile]
         )
 
     solid_copy = pltpu.make_async_copy(solid_hbm, solid, solid_sem)
     for side in range(2):
-        for copy in row_copies(side):
-            copy.start()
+        row_solid_copy(side).start()
+    for tile in range(4):
+        for side in range(2):
+            row_copy(side, tile).start()
     solid_copy.start()
-    for chunk in (0, 7, 1, 2):
-        chunk_copy(chunk).start()
+    for chunk in (0, 7, 1, 2, 3, 4, 5, 6):
+        for tile in range(4):
+            chunk_copy(chunk, tile).start()
     small_copies = (
         pltpu.make_async_copy(breakage_hbm, breakage, small_sem.at[0]),
         pltpu.make_async_copy(selection_hbm, selection, small_sem.at[1]),
@@ -291,17 +306,18 @@
 
     def prepare_y(tile, carry):
         for side in range(2):
+            row_copy(side, tile).wait()
             prepare(1, side, tile)
         return carry
 
     def prepare_x(tile, carry):
         for side in range(2):
+            chunk_copy(7 * (1 - side), tile).wait()
             prepare(0, side, tile)
         return carry
 
     for side in range(2):
-        for copy in row_copies(side):
-            copy.wait()
+        row_solid_copy(side).wait()
     lax.fori_loop(0, 4, prepare_y, 0)
 
     def ends_copy(side, end):
@@ -319,16 +335,16 @@
             ends_copy(side, end).start()
 
     solid_copy.wait()
-    for chunk in (0, 7):
-        chunk_copy(chunk).wait()
 
     lax.fori_loop(0, 4, prepare_x, 0)
 
-    def first_pass(chunk):
+    def first_pass(chunk, loaded):
         half = chunk // 4
 
         def one_tile(tile, carry):
-            lanes = pl.ds(pl.multiple_of(tile * 128, 128), 128)
+            if not loaded:
+                chunk_copy(chunk, tile).wait()
+            lanes = lanes_of(tile)
             heats = []
             for part in range(4):
                 plane, rows = 2 * chunk + part // 2, slice(8 * (part % 2), 8 * (part % 2) + 8)
@@ -356,38 +372,15 @@
         lax.fori_loop(0, 4, one_tile, 0)
 
     def outer_chunks(step, carry):
-        first_pass(step * 7)
+        first_pass(step * 7, True)
         return carry
 
     def inner_chunks(chunk, carry):
-        chunk_copy(chunk).wait()
-
-        @pl.when(chunk < 5)
-        def _():
-            chunk_copy(chunk + 2).start()
-
-        first_pass(chunk)
+        first_pass(chunk, False)
         return carry
 
     lax.fori_loop(0, 2, outer_chunks, 0)
-    lax.fori_loop(1, 7, inner_chunks, 0)
-
-    for tile in range(4):
-        sums_out[tile, 0:4, :] = jnp.sum(heat_acc[:, tile], axis=1)
-    sums_in[pl.ds(gy, 1)] = sums_out[pl.ds(gy // 2, 1)]
-
-    def sums_copy(d):
-        return pltpu.make_async_remote_copy(
-            src_ref=sums_out.at[peers[d] // 2],
-            dst_ref=sums_in.at[gy],
-            send_sem=sums_send.at[d],
-            recv_sem=sums_recv.at[d],
-            device_id=(gx, peers[d]),
-            device_id_type=MESH,
-        )
-
-    for d in range(1, ny):
-        sums_copy(d).start()
+    lax.fori_loop(1, EARLY, inner_chunks, 0)
 
     for d in range(1, ny):
         rate_copy(d).wait_recv()
@@ -448,16 +441,39 @@
                 place : place + 1
             ] + equilibrium_of(index, terms)
 
-    for place in (0, 3, 4, 1, 2):
-        for side in range(2):
+    for side in range(2):
+        for place in (0, 3, 4):
             leave(0, side, place)
-            if LEAVE_X[side][place] in CORNERS:
-                leave_corner(LEAVE_X[side][place])
+            edge_copy(0, side, place).start()
+
+    lax.fori_loop(EARLY, 7, inner_chunks, 0)
+
+    for side in range(2):
+        for place in (1, 2):
+            leave(0, side, place)
+            leave_corner(LEAVE_X[side][place])
             edge_copy(0, side, place).start()
     for place in range(5):
         for side in range(2):
             leave(1, side, place)
             edge_copy(1, side, place).start()
+
+    for tile in range(4):
+        sums_out[tile, 0:4, :] = jnp.sum(heat_acc[:, tile], axis=1)
+    sums_in[pl.ds(gy, 1)] = sums_out[pl.ds(gy // 2, 1)]
+
+    def sums_copy(d):
+        return pltpu.make_async_remote_copy(
+            src_ref=sums_out.at[peers[d] // 2],
+            dst_ref=sums_in.at[gy],
+            send_sem=sums_send.at[d],
+            recv_sem=sums_recv.at[d],
+            device_id=(gx, peers[d]),
+            device_id_type=MESH,
+        )
+
+    for d in range(1, ny):
+        sums_copy(d).start()
 
     def put(index, plane, tile, low, high):
         c = velocities[index]
@@ -586,11 +602,12 @@
             pltpu.VMEM((2, 2, 5, 16, 512), F32),
             pltpu.VMEM((2, 9, 16, 512), F32),
             pltpu.VMEM((2, 2, 9, 512), F32),
-            dma((8,)),
+            dma((8, 4)),
             dma,
             dma,
             dma((2,)),
-            dma((2, 2)),
+            dma((2,)),
+            dma((2, 4)),
             dma((8,)),
             dma((8,)),
             dma((8,)),

time: 26.4 us -> 27.3 us (1.034)
  Pallas kernels: 25.6 us -> 26.6 us
    pallas_call x1, Pallas kernels: 21.6 us -> 22.6 us  [per_device(): pl.pallas_call(functools.partial(step_kernel, nx, ny), out_shape=(pltpu.V...]
where the time goes in v6:
time: 27.3 us; the launch traced here: 27.2 us
  Pallas kernels  26.6 us (97%)
  between operations  0.64 us (2%)
    pallas_call x1, Pallas kernels, per_device(): pl.pallas_call(functools.partial(step_kernel, nx, ny), out_shape=(pltpu.V...  22.6 us
    pallas_call x1, Pallas kernels, per_device(): pl.pallas_call(finish_kernel, out_shape=(jax.ShapeDtypeStruct(populations...  3.95 us

profile of v6, /device:TPU:0, one launch (start us, length us, event | category | flops | bytes accessed | tf_op | source)
XLA Modules:
  0.0 27.2 jit_solution(18164162612174133126)
XLA Ops:
  0.6 22.6 %collide.1 = (f32[19,18,16,512]{3,2,1,0:T(8,128)S(1)}, f32[256,64]{1,0:T(8,128)S(1)}) custom-call(f32[19,16,16,512]{3,2,1,0:T(8,128)} %pop_hbm.1, s32[16,16,512]{2,1,0:T(8,128)} %solid_hbm.1, f32[256,64]{1,0:T(8,128)} %bitcast.6, f32[64,64]{1,0:T(8,128)} %breakage_hbm.1, f32[64]{0:T(128)} %selection_hbm.1), custom_call_target="tpu_custom_call" | custom-call | tf_op jit(solution)/shard_map/collide/pallas_call | solution.py:576
  23.2 3.9 %finish.1 = (f32[19,16,16,512]{3,2,1,0:T(8,128)}, f32[256,64]{1,0:T(8,128)}) custom-call(f32[19,18,16,512]{3,2,1,0:T(8,128)S(1)} %get-tuple-element.6.moved, f32[256,64]{1,0:T(8,128)S(1)} %get-tuple-element.7.result), custom_call_target="tpu_custom_call" | custom-call | tf_op jit(solution)/shard_map/finish/pallas_call | solution.py:630

commit v7 on v6

--- a/solution.py
+++ b/solution.py
@@ -448,6 +448,23 @@
 
     lax.fori_loop(EARLY, 7, inner_chunks, 0)
 
+    for tile in range(4):
+        sums_out[tile, 0:4, :] = jnp.sum(heat_acc[:, tile], axis=1)
+    sums_in[pl.ds(gy, 1)] = sums_out[pl.ds(gy // 2, 1)]
+
+    def sums_copy(d):
+        return pltpu.make_async_remote_copy(
+            src_ref=sums_out.at[peers[d] // 2],
+            dst_ref=sums_in.at[gy],
+            send_sem=sums_send.at[d],
+            recv_sem=sums_recv.at[d],
+            device_id=(gx, peers[d]),
+            device_id_type=MESH,
+        )
+
+    for d in range(1, ny):
+        sums_copy(d).start()
+
     for side in range(2):
         for place in (1, 2):
             leave(0, side, place)
@@ -457,23 +474,6 @@
         for side in range(2):
             leave(1, side, place)
             edge_copy(1, side, place).start()
-
-    for tile in range(4):
-        sums_out[tile, 0:4, :] = jnp.sum(heat_acc[:, tile], axis=1)
-    sums_in[pl.ds(gy, 1)] = sums_out[pl.ds(gy // 2, 1)]
-
-    def sums_copy(d):
-        return pltpu.make_async_remote_copy(
-            src_ref=sums_out.at[peers[d] // 2],
-            dst_ref=sums_in.at[gy],
-            send_sem=sums_send.at[d],
-            recv_sem=sums_recv.at[d],
-            device_id=(gx, peers[d]),
-            device_id_type=MESH,
-        )
-
-    for d in range(1, ny):
-        sums_copy(d).start()
 
     def put(index, plane, tile, low, high):
         c = velocities[index]

time: 27.3 us -> 26.6 us (0.974)
  Pallas kernels: 26.6 us -> 25.9 us
    pallas_call x1, Pallas kernels: 22.6 us -> 21.9 us  [per_device(): pl.pallas_call(functools.partial(step_kernel, nx, ny), out_shape=(pltpu.V...]
where the time goes in v7:
time: 26.6 us; the launch traced here: 26.5 us
  Pallas kernels  25.9 us (97%)
  between operations  0.64 us (2%)
    pallas_call x1, Pallas kernels, per_device(): pl.pallas_call(functools.partial(step_kernel, nx, ny), out_shape=(pltpu.V...  21.9 us
    pallas_call x1, Pallas kernels, per_device(): pl.pallas_call(finish_kernel, out_shape=(jax.ShapeDtypeStruct(populations...  3.95 us

profile of v7, /device:TPU:0, one launch (start us, length us, event | category | flops | bytes accessed | tf_op | source)
XLA Modules:
  0.0 26.5 jit_solution(4071186623616508418)
XLA Ops:
  0.6 21.9 %collide.1 = (f32[19,18,16,512]{3,2,1,0:T(8,128)S(1)}, f32[256,64]{1,0:T(8,128)S(1)}) custom-call(f32[19,16,16,512]{3,2,1,0:T(8,128)} %pop_hbm.1, s32[16,16,512]{2,1,0:T(8,128)} %solid_hbm.1, f32[256,64]{1,0:T(8,128)} %bitcast.6, f32[64,64]{1,0:T(8,128)} %breakage_hbm.1, f32[64]{0:T(128)} %selection_hbm.1), custom_call_target="tpu_custom_call" | custom-call | tf_op jit(solution)/shard_map/collide/pallas_call | solution.py:576
  22.6 3.9 %finish.1 = (f32[19,16,16,512]{3,2,1,0:T(8,128)}, f32[256,64]{1,0:T(8,128)}) custom-call(f32[19,18,16,512]{3,2,1,0:T(8,128)S(1)} %get-tuple-element.6.moved, f32[256,64]{1,0:T(8,128)S(1)} %get-tuple-element.7.result), custom_call_target="tpu_custom_call" | custom-call | tf_op jit(solution)/shard_map/finish/pallas_call | solution.py:630

commit v8 on v4

--- a/solution.py
+++ b/solution.py
@@ -150,6 +150,7 @@
     pop_sem,
     solid_sem,
     counts_sem,
+    row_solid_sem,
     row_sem,
     rate_send,
     rate_recv,
@@ -176,24 +177,37 @@
     for partner in partners:
         pl.semaphore_signal(barrier, inc=1, device_id=partner, device_id_type=MESH)
 
-    def chunk_copy(chunk):
-        rows = pl.ds(2 * chunk, 2)
-        return pltpu.make_async_copy(pop_hbm.at[:, rows], pops.at[:, rows], pop_sem.at[chunk])
-
-    def row_copies(side):
+    def lanes_of(tile):
+        return pl.ds(pl.multiple_of(tile * 128, 128), 128)
+
+    def chunk_copy(chunk, tile):
+        rows, lanes = pl.ds(2 * chunk, 2), lanes_of(tile)
+        return pltpu.make_async_copy(
+            pop_hbm.at[:, rows, :, lanes], pops.at[:, rows, :, lanes], pop_sem.at[chunk, tile]
+        )
+
+    def row_solid_copy(side):
         y = 15 if side == 0 else 0
-        return (
-            pltpu.make_async_copy(solid_hbm.at[:, y], row_solid.at[side], row_sem.at[side, 0]),
-            pltpu.make_async_copy(pop_hbm.at[:, :, y], row_pops.at[side], row_sem.at[side, 1]),
+        return pltpu.make_async_copy(
+            solid_hbm.at[:, y], row_solid.at[side], row_solid_sem.at[side]
+        )
+
+    def row_copy(side, tile):
+        y, lanes = 15 if side == 0 else 0, lanes_of(tile)
+        return pltpu.make_async_copy(
+            pop_hbm.at[:, :, y, lanes], row_pops.at[side, :, :, lanes], row_sem.at[side, tile]
         )
 
     solid_copy = pltpu.make_async_copy(solid_hbm, solid, solid_sem)
     for side in range(2):
-        for copy in row_copies(side):
-            copy.start()
+        row_solid_copy(side).start()
+    for tile in range(4):
+        for side in range(2):
+            row_copy(side, tile).start()
     solid_copy.start()
-    for chunk in (0, 7, 1, 2):
-        chunk_copy(chunk).start()
+    for chunk in (0, 7, 1, 2, 3, 4, 5, 6):
+        for tile in range(4):
+            chunk_copy(chunk, tile).start()
 
     counts_copy.wait()
     row, lane = iota((256, 128), 0), iota((256, 128), 1)
@@ -206,12 +220,28 @@
     rate_out[...] = (1.0 / relax_time(load)).reshape(8, 8, 128)
     rate_in[pl.ds(gy, 1)] = rate_out[pl.ds(gy, 1)]
 
+    pl.semaphore_wait(barrier, len(partners))
+
+    def rate_copy(d):
+        return pltpu.make_async_remote_copy(
+            src_ref=rate_out.at[peers[d]],
+            dst_ref=rate_in.at[gy],
+            send_sem=rate_send.at[d],
+            recv_sem=rate_recv.at[d],
+            device_id=(gx, peers[d]),
+            device_id_type=MESH,
+        )
+
+    for d in range(1, ny):
+        rate_copy(d).start()
+
     heat_acc[...] = jnp.zeros_like(heat_acc)
     sums_out[...] = jnp.zeros_like(sums_out)
 
     def prepare_y(tile, carry):
-        lanes = pl.ds(pl.multiple_of(tile * 128, 128), 128)
+        lanes = lanes_of(tile)
         for side in range(2):
+            row_copy(side, tile).wait()
             for part in range(2):
                 rows = slice(8 * part, 8 * part + 8)
                 f = [row_pops[side, index, rows, lanes] for index in range(19)]
@@ -236,24 +266,8 @@
         )
 
     for side in range(2):
-        for copy in row_copies(side):
-            copy.wait()
+        row_solid_copy(side).wait()
     lax.fori_loop(0, 4, prepare_y, 0)
-
-    pl.semaphore_wait(barrier, len(partners))
-
-    def rate_copy(d):
-        return pltpu.make_async_remote_copy(
-            src_ref=rate_out.at[peers[d]],
-            dst_ref=rate_in.at[gy],
-            send_sem=rate_send.at[d],
-            recv_sem=rate_recv.at[d],
-            device_id=(gx, peers[d]),
-            device_id_type=MESH,
-        )
-
-    for d in range(1, ny):
-        rate_copy(d).start()
 
     def ends_copy(side, end):
         return pltpu.make_async_remote_copy(
@@ -274,6 +288,7 @@
     def prepare_x(tile, carry):
         lanes = pl.ds(pl.multiple_of(tile * 128, 128), 128)
         for side in range(2):
+            chunk_copy(7 * (1 - side), tile).wait()
             plane = 15 if side == 0 else 0
             for part in range(2):
                 rows = slice(8 * part, 8 * part + 8)
@@ -292,16 +307,16 @@
         return carry
 
     solid_copy.wait()
-    for chunk in (0, 7):
-        chunk_copy(chunk).wait()
 
     lax.fori_loop(0, 4, prepare_x, 0)
 
-    def first_pass(chunk):
+    def first_pass(chunk, loaded):
         half = chunk // 4
 
         def one_tile(tile, carry):
-            lanes = pl.ds(pl.multiple_of(tile * 128, 128), 128)
+            if not loaded:
+                chunk_copy(chunk, tile).wait()
+            lanes = lanes_of(tile)
             heats = []
             for part in range(4):
                 plane, rows = 2 * chunk + part // 2, slice(8 * (part % 2), 8 * (part % 2) + 8)
@@ -329,17 +344,11 @@
         lax.fori_loop(0, 4, one_tile, 0)
 
     def outer_chunks(step, carry):
-        first_pass(step * 7)
+        first_pass(step * 7, True)
         return carry
 
     def inner_chunks(chunk, carry):
-        chunk_copy(chunk).wait()
-
-        @pl.when(chunk < 5)
-        def _():
-            chunk_copy(chunk + 2).start()
-
-        first_pass(chunk)
+        first_pass(chunk, False)
         return carry
 
     lax.fori_loop(0, 2, outer_chunks, 0)
@@ -629,10 +638,11 @@
             pltpu.VMEM((2, 9, 16, 512), F32),
             pltpu.VMEM((2, 9, 16, 512), F32),
             pltpu.VMEM((2, 2, 9, 512), F32),
-            dma((8,)),
+            dma((8, 4)),
             dma,
             dma,
-            dma((2, 2)),
+            dma((2,)),
+            dma((2, 4)),
             dma((8,)),
             dma((8,)),
             dma((8,)),

time: 26.4 us -> 26.7 us (1.011)
  Pallas kernels: 25.5 us -> 25.9 us
    pallas_call x1, Pallas kernels: 21.3 us -> 21.7 us  [per_device(): pl.pallas_call(functools.partial(step_kernel, nx, ny), out_shape=(pltpu.V...]
where the time goes in v8:
time: 26.7 us; the launch traced here: 26.6 us
  Pallas kernels  25.9 us (97%)
  between operations  0.69 us (3%)
    pallas_call x1, Pallas kernels, per_device(): pl.pallas_call(functools.partial(step_kernel, nx, ny), out_shape=(pltpu.V...  21.7 us
    pallas_call x1, Pallas kernels, per_device(): pl.pallas_call(finish_kernel, out_shape=(jax.ShapeDtypeStruct(populations...  4.19 us

profile of v8, /device:TPU:0, one launch (start us, length us, event | category | flops | bytes accessed | tf_op | source)
XLA Modules:
  0.0 26.6 jit_solution(12851869349365335231)
XLA Ops:
  0.6 0.0 copy-start.2
  0.6 0.0 copy-start.1
  0.7 0.0 copy-start
  0.7 21.7 %collide.1 = (f32[19,18,16,512]{3,2,1,0:T(8,128)S(1)}, f32[2,5,16,512]{3,2,1,0:T(8,128)S(1)}, f32[8,8,128]{2,1,0:T(8,128)S(1)}) custom-call(f32[19,16,16,512]{3,2,1,0:T(8,128)} %pop_hbm.1, s32[16,16,512]{2,1,0:T(8,128)} %solid_hbm.1, f32[256,64]{1,0:T(8,128)} %bitcast.6), custom_call_target="tpu_custom_call" | custom-call | tf_op jit(solution)/shard_map/collide/pallas_call | solution.py:613
  22.3 0.0 copy-done.2
  22.4 0.0 copy-done.1
  22.4 0.0 copy-done
  22.4 4.2 %finish.1 = (f32[19,16,16,512]{3,2,1,0:T(8,128)}, f32[256,64]{1,0:T(8,128)}) custom-call(f32[19,18,16,512]{3,2,1,0:T(8,128)S(1)} %get-tuple-element.7.moved, f32[2,5,16,512]{3,2,1,0:T(8,128)S(1)} %get-tuple-element.8.y_rows, f32[8,8,128]{2,1,0:T(8,128)S(1)} %get-tuple-element.9.sums_in, f32[256,64]{1,0:T(8,128)S(1)} %bitcast.7, f32[64,64]{1,0:T(8,128)S(1)} %copy-done.1, ...), custom_call_target="tpu_custom_call" | custom-call | tf_op jit(solution)/shard_map/finish/pallas_call | solution.py:662
Async XLA Ops:
  0.6 21.7 %copy-start.2 = (f32[64]{0:T(128)S(1)}, f32[64]{0:T(128)}, u32[]{:S(2)}) copy-start(f32[64]{0:T(128)} %selection_hbm.1) | copy-start | bytes 772
  0.6 21.7 %copy-start.1 = (f32[64,64]{1,0:T(8,128)S(1)}, f32[64,64]{1,0:T(8,128)}, u32[]{:S(2)}) copy-start(f32[64,64]{1,0:T(8,128)} %breakage_hbm.1) | copy-start | bytes 49156
  0.7 21.7 %copy-start = (f32[64,2,16,8]{0,3,2,1:T(8,128)S(1)}, f32[64,2,16,8]{0,3,2,1:T(8,128)}, u32[]{:S(2)}) copy-start(f32[64,2,16,8]{0,3,2,1:T(8,128)} %param.7) | copy-start | bytes 196612

commit v9 on v3

--- a/solution.py
+++ b/solution.py
@@ -331,6 +331,23 @@
     lax.fori_loop(0, 2, outer_chunks, 0)
     lax.fori_loop(1, 7, inner_chunks, 0)
 
+    for tile in range(4):
+        sums_out[tile, 0:4, :] = jnp.sum(heat_acc[:, tile], axis=1)
+    sums_in[pl.ds(gy, 1)] = sums_out[pl.ds(gy // 2, 1)]
+
+    def sums_copy(d):
+        return pltpu.make_async_remote_copy(
+            src_ref=sums_out.at[peers[d] // 2],
+            dst_ref=sums_in.at[gy],
+            send_sem=sums_send.at[d],
+            recv_sem=sums_recv.at[d],
+            device_id=(gx, peers[d]),
+            device_id_type=MESH,
+        )
+
+    for d in range(1, ny):
+        sums_copy(d).start()
+
     for d in range(1, ny):
         rate_copy(d).wait_recv()
     lane = iota((8, 128), 1)
@@ -385,23 +402,6 @@
                 if corner[0] == LEAVE_X[side][place]:
                     corner_copy(slot).start()
             edge_copy(side, place).start()
-
-    for tile in range(4):
-        sums_out[tile, 0:4, :] = jnp.sum(heat_acc[:, tile], axis=1)
-    sums_in[pl.ds(gy, 1)] = sums_out[pl.ds(gy // 2, 1)]
-
-    def sums_copy(d):
-        return pltpu.make_async_remote_copy(
-            src_ref=sums_out.at[peers[d] // 2],
-            dst_ref=sums_in.at[gy],
-            send_sem=sums_send.at[d],
-            recv_sem=sums_recv.at[d],
-            device_id=(gx, peers[d]),
-            device_id_type=MESH,
-        )
-
-    for d in range(1, ny):
-        sums_copy(d).start()
 
     def put(index, plane, tile, low, high):
         c = velocities[index]

time: 25.7 us -> 25.8 us (level)
  no operation moved by 1% of the time
where the time goes in v9:
time: 25.8 us; the launch traced here: 25.6 us
  Pallas kernels  24.9 us (97%)
  between operations  0.69 us (3%)
    pallas_call x1, Pallas kernels, per_device(): pl.pallas_call(functools.partial(step_kernel, nx, ny), out_shape=(pltpu.V...  20.7 us
    pallas_call x1, Pallas kernels, per_device(): pl.pallas_call(finish_kernel, out_shape=(jax.ShapeDtypeStruct(populations...  4.19 us

profile of v9, /device:TPU:0, one launch (start us, length us, event | category | flops | bytes accessed | tf_op | source)
XLA Modules:
  0.0 25.6 jit_solution(11763278449134202681)
XLA Ops:
  0.6 0.0 copy-start.2
  0.6 0.0 copy-start.1
  0.7 0.0 copy-start
  0.7 20.7 %collide.1 = (f32[19,18,16,512]{3,2,1,0:T(8,128)S(1)}, f32[2,5,16,512]{3,2,1,0:T(8,128)S(1)}, f32[8,8,128]{2,1,0:T(8,128)S(1)}) custom-call(f32[19,16,16,512]{3,2,1,0:T(8,128)} %pop_hbm.1, s32[16,16,512]{2,1,0:T(8,128)} %solid_hbm.1, f32[256,64]{1,0:T(8,128)} %bitcast.6), custom_call_target="tpu_custom_call" | custom-call | tf_op jit(solution)/shard_map/collide/pallas_call | solution.py:588
  21.4 0.0 copy-done.2
  21.4 0.0 copy-done.1
  21.4 0.0 copy-done
  21.4 4.2 %finish.1 = (f32[19,16,16,512]{3,2,1,0:T(8,128)}, f32[256,64]{1,0:T(8,128)}) custom-call(f32[19,18,16,512]{3,2,1,0:T(8,128)S(1)} %get-tuple-element.7.moved, f32[2,5,16,512]{3,2,1,0:T(8,128)S(1)} %get-tuple-element.8.y_rows, f32[8,8,128]{2,1,0:T(8,128)S(1)} %get-tuple-element.9.sums_in, f32[256,64]{1,0:T(8,128)S(1)} %bitcast.7, f32[64,64]{1,0:T(8,128)S(1)} %copy-done.1, ...), custom_call_target="tpu_custom_call" | custom-call | tf_op jit(solution)/shard_map/finish/pallas_call | solution.py:636
Async XLA Ops:
  0.6 20.7 %copy-start.2 = (f32[64]{0:T(128)S(1)}, f32[64]{0:T(128)}, u32[]{:S(2)}) copy-start(f32[64]{0:T(128)} %selection_hbm.1) | copy-start | bytes 772
  0.6 20.7 %copy-start.1 = (f32[64,64]{1,0:T(8,128)S(1)}, f32[64,64]{1,0:T(8,128)}, u32[]{:S(2)}) copy-start(f32[64,64]{1,0:T(8,128)} %breakage_hbm.1) | copy-start | bytes 49156
  0.7 20.7 %copy-start = (f32[64,2,16,8]{0,3,2,1:T(8,128)S(1)}, f32[64,2,16,8]{0,3,2,1:T(8,128)}, u32[]{:S(2)}) copy-start(f32[64,2,16,8]{0,3,2,1:T(8,128)} %param.7) | copy-start | bytes 196612
